TPU v7x, 256 devices: a whole 4x4x8 slice. The times are simulated.
256 devices in a mesh: occ: 4 (over x_lo, core), vir: 16 (over z, x_hi), rep: 4 (over y).
Axes of the slice: x: 4 (x_hi: 2, x_lo: 2; x = x_hi * 2 + x_lo), y: 4, z: 8, core: 2. Of those that a mesh axis runs over, the one named last changes fastest.
Arguments:
- integrals: float32 [8192, 16384], P('vir', 'rep'), may hold values from -0.046875 to 0.046875
- amplitudes: float32 [16384, 4096], P(('rep', 'vir'), 'occ'), may hold values from -6 to 6
Outputs:
- ladder: float32 [8192, 4096], P('vir', ('occ', 'rep'))
All inputs are finite; a program needn't handle non-finite values.
Results may differ from a plain program's by a relative error of at most 0.00007.
Values sent between devices are 32-bit elements; how exact they have to be, the bound alone decides.
No kernel may reach another device: no remote copies, remote signals or barrier semaphores. Data moves between devices by JAX's collectives and lax.ppermute only.
A program may use at most 128 MiB of HBM per device.

v0:
```python
import functools

import jax
import jax.numpy as jnp
import numpy as np
from jax import lax
from jax.experimental import pallas as pl
from jax.experimental.pallas import tpu as pltpu
from jax.sharding import Mesh, PartitionSpec as P

O = 64
GROUP = ("xl", "c", "y")
F32, BF16 = jnp.float32, jnp.bfloat16
VMEM_PRODUCT = 57 * 2**20


def quad_partners(o, a, p):
    return (a, a ^ 2) if o < (o ^ p) else (a ^ 1, a ^ 3)


def own_pairs(o, a):
    g = 4 * o + a
    h = 4 * o + (a + 1) % 4
    out = [(4 * g + s, 4 * h + t) for s in range(4) for t in range(4)]
    h = 4 * o + (a ^ 2)
    if a < (a ^ 2):
        out += [(4 * g + s, 4 * h + t) for s in (0, 1) for t in range(4)]
    else:
        out += [(4 * g + s, 4 * h + t) for t in (2, 3) for s in range(4)]
    out += [(4 * g + s, 4 * g + t) for s in range(4) for t in range(s + 1, 4)]
    out += [None, None]
    lists = [out]
    for p in (1, 2, 3):
        lists.append([(4 * g + s, 4 * (4 * (o ^ p) + b) + t) for b in quad_partners(o, a, p) for s in range(4) for t in range(4)])
    return lists


def select_table():
    table = -np.ones((4, 2, 896), np.int32)
    for o in range(4):
        for a in range(4):
            for p, pairs in enumerate(own_pairs(o, a)):
                for k, pair in enumerate(pairs):
                    if pair is None:
                        continue
                    i, j = pair
                    at = p * 128 + a * 32 + k
                    table[o, 0, at] = (i - 16 * o) * O + j
                    if p == 0:
                        table[o, 1, at] = (j - 16 * o) * O + i
            for p in (1, 2, 3):
                for k, (j, i) in enumerate(own_pairs(o ^ p, a)[p]):
                    table[o, 0, 512 + (p - 1) * 128 + a * 32 + k] = (i - 16 * o) * O + j
    return table


def send_perms():
    quads = [(o, a) for o in range(4) for a in range(4)]
    perms = [
        (range(0, 16), [(4 * o + a, 4 * o + (a + 1) % 4) for o, a in quads]),
        (range(16, 24), [(4 * o + a, 4 * o + (a ^ 2)) for o, a in quads]),
    ]
    for p in (1, 2, 3):
        for t in (0, 1):
            start = 32 * p + 16 * t
            perms.append((range(start, start + 16), [(4 * o + a, 4 * (o ^ p) + quad_partners(o, a, p)[t]) for o, a in quads]))
    return perms


def expand_table():
    own = [sum(own_pairs(g // 4, g % 4), []) for g in range(16)]
    table = np.zeros((16, 2, 256), np.int32)
    table[:, 0] = -1
    held = [list(own[g]) for g in range(16)]
    for slots, perm in send_perms():
        for source, target in perm:
            held[target] += [own[source][s] for s in slots]
    for g in range(16):
        for slot, pair in enumerate(held[g]):
            if pair is None:
                continue
            for (i, j), sign in ((pair, 1), (pair[::-1], -1)):
                if i // 4 == g:
                    table[g, :, (i - 4 * g) * O + j] = slot, sign
        assert sum(table[g, 0] < 0) == 4
    return table


def parts_of(x, n):
    parts = []
    for _ in range(n):
        part = x.astype(BF16)
        parts.append(part)
        x = x - part.astype(F32)
    return parts


def call(body, out, *args, scratch=(), smem=(), vmem=16 * 2**20, anywhere=(), after=(), flops=0):
    spaces = [pltpu.SMEM if k in smem else pl.ANY if k in anywhere else pltpu.VMEM for k in range(len(args))]
    count = len(args)

    def without_after(*refs):
        body(*refs[:count], *refs[count + len(after):])

    return pl.pallas_call(
        without_after,
        out_shape=out,
        in_specs=[pl.BlockSpec(memory_space=m) for m in spaces + [pl.ANY] * len(after)],
        out_specs=[pl.BlockSpec(memory_space=pltpu.VMEM)] * len(out),
        scratch_shapes=list(scratch),
        compiler_params=pltpu.CompilerParams(vmem_limit_bytes=vmem),
        cost_estimate=pl.CostEstimate(flops=flops, bytes_accessed=0, transcendentals=0),
    )(*args, *after)


def in_step(value, after):
    def body(source, target):
        target[...] = source[...]

    return call(body, [jax.ShapeDtypeStruct(value.shape, value.dtype)], value, after=after)[0]


def f32(*shape):
    return jax.ShapeDtypeStruct(shape, F32)


def select_body(occ_ref, table_ref, b_ref, *outs):
    kept, sent1, sent2, sent3 = outs
    parts = parts_of(b_ref[...], 2)
    for n, (ref, lo, p) in enumerate([
        (sent1, 0, 4), (sent2, 0, 5), (sent3, 0, 6), (kept, 0, 0), (kept, 128, 1), (kept, 256, 2), (kept, 384, 3)]):
        cols = slice(p * 128, p * 128 + 128)
        row = lax.broadcasted_iota(jnp.int32, (b_ref.shape[1], 128), 0)
        hot = jnp.where(row == table_ref[occ_ref[0], 0:1, cols], 1.0, 0.0)
        if p == 0:
            hot = hot - jnp.where(row == table_ref[occ_ref[0], 1:2, cols], 1.0, 0.0)
        hot = hot.astype(BF16)
        acc = jnp.dot(parts[0], hot, preferred_element_type=F32)
        for part in parts[1:]:
            acc += jnp.dot(part, hot, preferred_element_type=F32)
        ref[:, lo:lo + 128] = acc


def sub_body(x_ref, *refs):
    o_ref = refs[-1]
    width = x_ref.shape[1]
    first = width - 128 * (len(refs) - 1)
    if first:
        o_ref[:, :first] = x_ref[:, :first]
    for k, ref in enumerate(refs[:-1]):
        at = slice(first + 128 * k, first + 128 * k + 128)
        o_ref[:, at] = x_ref[:, at] - ref[...]


def product_body(places, has_total, last, at_ref, a_ref, *refs):
    refs = list(refs)
    blocks = [refs.pop(0) for _ in places]
    before = refs.pop(0) if has_total else None
    outs = [refs.pop(0) for _ in range(8 if last else 1)]
    held, sems, a_parts, b_parts, turned = refs
    depth, width = blocks[0].shape
    copies = []
    for n, (up, other) in enumerate(places):
        block = 2 * ((at_ref[1] + up) % 8) + (at_ref[2] + other) % 2
        cols = pl.ds(pl.multiple_of(block * depth, depth), depth)
        copies.append(pltpu.make_async_copy(a_ref.at[:, cols], held.at[n], sems.at[n]))
        copies[-1].start()
    for n, block in enumerate(blocks):
        hi, lo = parts_of(block[...], 2)
        for m, part in enumerate((hi, hi, lo)):
            b_parts[(3 * n + m) * depth:(3 * n + m + 1) * depth, :] = part
    for n, copy in enumerate(copies):
        copy.wait()
        hi, lo = parts_of(held[n], 2)
        for m, part in enumerate((hi, lo, hi)):
            a_parts[:, (3 * n + m) * depth:(3 * n + m + 1) * depth] = part
    tile = 256
    for m in range(held.shape[1] // tile):
        rows = slice(m * tile, (m + 1) * tile)
        for n in range(width // tile):
            cols = slice(n * tile, (n + 1) * tile)
            total = jnp.dot(a_parts[rows, :], b_parts[:, cols], preferred_element_type=F32)
            if has_total:
                total += before[rows, cols]
            if last:
                turned[cols, rows] = total.T
            else:
                outs[0][rows, cols] = total
    if last:
        for r in range(4):
            first = ((at_ref[0] + r) % 4) * 32
            for p in range(4):
                outs[r + p // 2 * 4][p % 2 * 32:p % 2 * 32 + 32, :] = turned[pl.ds(pl.multiple_of(p * 128 + first, 32), 32), :]


def sum_body(a, b, c, d, o):
    o[...] = (a[...] + b[...]) + (c[...] + d[...])


def pair_body(cuts, a, b, o, *sends):
    value = a[...] - b[...]
    o[...] = value
    for (first, count), ref in zip(cuts, sends):
        ref[...] = value[first:first + count, :]


def expand_body(quad_ref, table_ref, *refs):
    *ins, o_ref, held = refs
    at = 0
    for ref in ins:
        held[at:at + ref.shape[0], :] = ref[...]
        at += ref.shape[0]
    held[at:, :] = jnp.zeros((held.shape[0] - at, held.shape[1]), F32)
    row = lax.broadcasted_iota(jnp.int32, (held.shape[0], o_ref.shape[1]), 0)
    table = table_ref[quad_ref[0]]
    hot = jnp.where(row == table[0:1, :], table[1:2, :].astype(F32), 0.0).astype(BF16)
    turned = held[...].T
    acc = None
    for part in parts_of(turned, 3):
        term = jnp.dot(part, hot, preferred_element_type=F32)
        acc = term if acc is None else acc + term
    o_ref[...] = acc


def moved_along(value, axis, step):
    n = lax.axis_size(axis)
    return lax.ppermute(value, axis, [(k, (k + step) % n) for k in range(n)])


def flipped(value, axes, mask):
    n = lax.axis_size(axes)
    return lax.ppermute(value, axes, [(k, k ^ mask) for k in range(n)])


STEPS = (
    ((0, 0), (0, 0), (0, 0)),
    ((-1, 0), (1, 0), (1, 0)),
    ((-2, 0), (2, 0), (2, 0)),
    ((-3, 0), (2, 1), (-2, 0)),
    ((-2, 1), (3, 1), (-1, 0)),
)


def gather_step(held, step):
    up, down, across = STEPS[step]
    held[up[0] - 1, up[1]] = moved_along(held[up], "z", 1)
    held[down[0] + 1, down[1]] = moved_along(held[down], "z", -1)
    held[across[0], 1] = flipped(held[across], "xh", 1)
    return (up[0] - 1, up[1]), (down[0] + 1, down[1]), (across[0], 1)


def shards(integrals, amplitudes):
    xl, c, z, xh, y = (lax.axis_index(n) for n in ("xl", "c", "z", "xh", "y"))
    occ = 2 * xl + c
    quad = (4 * occ + y)[None]
    at = jnp.stack([y, z, xh])

    k = amplitudes.shape[0]
    kept, sent1, sent2, sent3 = call(
        select_body, [f32(k, 512), f32(k, 128), f32(k, 128), f32(k, 128)],
        occ[None], jnp.asarray(select_table()), amplitudes, smem=(0,))
    arrived = [flipped(value, ("xl", "c"), p) for p, value in ((1, sent1), (2, sent2), (3, sent3))]
    (unique,) = call(sub_body, [f32(k, 512)], kept, *arrived)

    def product(held, places, total, last):
        n = len(places)
        args = (at, integrals, *[held[p] for p in places]) + ((total,) if total is not None else ())
        out = [f32(64, 512)] * 8 if last else [f32(512, 512)]
        return call(functools.partial(product_body, places, total is not None, last), out, *args, smem=(0,), anywhere=(1,),
                    scratch=[pltpu.VMEM((n, 512, k), F32), pltpu.SemaphoreType.DMA((n,)), pltpu.VMEM((512, 3 * n * k), BF16),
                             pltpu.VMEM((3 * n * k, 512), BF16), pltpu.VMEM((512, 512), F32)],
                    vmem=VMEM_PRODUCT, flops=2 * 512 * n * k * 512 * 3)

    held = {(0, 0): unique}
    places, total = [(0, 0)], None
    ready = ()
    for step in range(5):
        down = STEPS[step][1]
        if step:
            held[down] = in_step(held[down], ready)
        arrived = gather_step(held, step)
        ready = (held[arrived[2]],)
        if step:
            (total,) = product(held, tuple(places), total, False)
            ready += (total,)
            places = []
        places += arrived
    total = product(held, tuple(places), total, True)

    perms = send_perms()
    pairs, arrived = [], []
    for n, pieces in enumerate((total[:4], total[4:])):
        moved = [moved_along(pieces[r], "y", r) for r in (1, 2, 3)]
        (mine,) = call(sum_body, [f32(64, 512)], pieces[0], *moved)
        lots = perms[4 * n:4 * n + 4]
        cuts = [(slots[0] - 64 * n, len(slots)) for slots, _ in lots]
        pair, *sends = call(functools.partial(pair_body, cuts), [f32(64, 512)] + [f32(count, 512) for _, count in cuts],
                            mine, moved_along(mine, "z", 4))
        pairs.append(pair)
        arrived += [lax.ppermute(value, GROUP, perm) for value, (_, perm) in zip(sends, lots)]
    (ladder,) = call(expand_body, [f32(512, 256)], quad, jnp.asarray(expand_table()), *pairs, *arrived,
                     scratch=[pltpu.VMEM((256, 512), F32)], smem=(0,))
    return ladder


def solution(mesh):
    fine = Mesh(mesh.devices.reshape(2, 2, 8, 2, 4), ("xl", "c", "z", "xh", "y"))
    in_specs = (P(("z", "xh"), "y"), P(("y", "z", "xh"), ("xl", "c")))
    out_specs = P(("z", "xh"), ("xl", "c", "y"))
    return jax.shard_map(shards, mesh=fine, in_specs=in_specs, out_specs=out_specs, check_vma=False)
```

profile of v0, /device:TPU:1, one launch (start us, length us, event | category | flops | bytes accessed | tf_op | source)
XLA Modules:
  0.0 142.7 jit_solution(2765945969801987989)
XLA Ops:
  2.0 2.3 %shard_map.46 = (f32[256,512]{1,0:T(8,128)S(1)}, f32[256,128]{1,0:T(8,128)S(1)}, f32[256,128]{1,0:T(8,128)S(1)}, f32[256,128]{1,0:T(8,128)S(1)}) custom-call(s32[1]{0:T(128)} %bitcast.4.refs_0_, s32[4,2,896]{2,1,0:T(2,128)S(1)} %copy-done.15, f32[256,1024]{1,0:T(8,128)S(1)} %copy-done.11), custom_call_target="tpu_custom_call" | custom-call | tf_op jit(solution)/shard_map/pallas_call | solution.py:105
  4.3 3.3 %collective-permute-start = (f32[256,128]{1,0:T(8,128)S(1)}, f32[256,128]{1,0:T(8,128)S(1)}, u32[]{:S(2)}, u32[]{:S(2)}) collective-permute-start(f32[256,128]{1,0:T(8,128)S(1)} %get-tuple-element.28), channel_id=1, source_target_pairs={{0,64},{64,0},{128,192},{192,128},{1,65},{65,1},{129,193},{193,129... | collective-permute-start | bytes 393224 | tf_op jit(solution)/shard_map/ppermute | solution.py:232
  7.6 1.7 %collective-permute-start.2 = (f32[256,128]{1,0:T(8,128)S(1)}, f32[256,128]{1,0:T(8,128)S(1)}, u32[]{:S(2)}, u32[]{:S(2)}) collective-permute-start(f32[256,128]{1,0:T(8,128)S(1)} %get-tuple-element.30), channel_id=1, source_target_pairs={{0,192},{64,128},{128,64},{192,0},{1,193},{65,129},{129,65},{193,1... | collective-permute-start | bytes 393224 | tf_op jit(solution)/shard_map/ppermute | solution.py:232
  9.4 3.3 %collective-permute-done.1.refs_2_ = f32[256,128]{1,0:T(8,128)S(1)} collective-permute-done((f32[256,128]{1,0:T(8,128)S(1)}, f32[256,128]{1,0:T(8,128)S(1)}, u32[]{:S(2)}, u32[]{:S(2)}) %collective-permute-start.1) | collective-permute-done | bytes 131104 | tf_op jit(solution)/shard_map/ppermute | solution.py:232
  12.7 3.0 %collective-permute-done.2.refs_3_ = f32[256,128]{1,0:T(8,128)S(1)} collective-permute-done((f32[256,128]{1,0:T(8,128)S(1)}, f32[256,128]{1,0:T(8,128)S(1)}, u32[]{:S(2)}, u32[]{:S(2)}) %collective-permute-start.2) | collective-permute-done | bytes 131104 | tf_op jit(solution)/shard_map/ppermute | solution.py:232
  16.8 5.6 %collective-permute-start.7 = (f32[256,512]{1,0:T(8,128)S(1)}, f32[256,512]{1,0:T(8,128)S(1)}, u32[]{:S(2)}, u32[]{:S(2)}) collective-permute-start(f32[256,512]{1,0:T(8,128)S(1)} %shard_map.47.refs_2_), channel_id=1, source_target_pairs={{0,56},{8,0},{16,8},{24,16},{32,24},{40,32},{48,40},{56,48},{1,57}... | collective-permute-start | bytes 1572872 | tf_op jit(solution)/shard_map/ppermute | solution.py:227
  22.4 8.2 %collective-permute-done.8.refs_1_.refs_5_ = f32[256,512]{1,0:T(8,128)S(1)} collective-permute-done((f32[256,512]{1,0:T(8,128)S(1)}, f32[256,512]{1,0:T(8,128)S(1)}, u32[]{:S(2)}, u32[]{:S(2)}) %collective-permute-start.8) | collective-permute-done | bytes 524320 | tf_op jit(solution)/shard_map/ppermute | solution.py:232
  30.7 2.6 %collective-permute-done.7.refs_0_ = f32[256,512]{1,0:T(8,128)S(1)} collective-permute-done((f32[256,512]{1,0:T(8,128)S(1)}, f32[256,512]{1,0:T(8,128)S(1)}, u32[]{:S(2)}, u32[]{:S(2)}) %collective-permute-start.7) | collective-permute-done | bytes 524320 | tf_op jit(solution)/shard_map/ppermute | solution.py:227
  33.6 3.8 %collective-permute-start.9 = (f32[256,512]{1,0:T(8,128)S(1)}, f32[256,512]{1,0:T(8,128)S(1)}, u32[]{:S(2)}, u32[]{:S(2)}) collective-permute-start(f32[256,512]{1,0:T(8,128)S(1)} %shard_map.48.refs_4_), channel_id=1, source_target_pairs={{0,56},{8,0},{16,8},{24,16},{32,24},{40,32},{48,40},{56,48},{1,57}... | collective-permute-start | bytes 1572872 | tf_op jit(solution)/shard_map/ppermute | solution.py:227
  38.8 5.9 %shard_map.49.refs_2_.refs_5_ = f32[512,512]{1,0:T(8,128)} custom-call(s32[3]{0:T(128)} %pad_add_fusion.refs_0_, f32[512,4096]{1,0:T(8,128)} %refs_1_.11, f32[256,512]{1,0:T(8,128)} %copy-done.10, f32[256,512]{1,0:T(8,128)} %copy-done.16, f32[256,512]{1,0:T(8,128)} %copy-done.7, f32[256,512]{1,0:T(8,128)} %copy-done.5), custom_call_target="tpu_custom_call" | custom-call | flops 1610612736 | tf_op jit(solution)/shard_map/pallas_call | solution.py:105
  44.7 2.2 %collective-permute-done.10.refs_1_.refs_4_ = f32[256,512]{1,0:T(8,128)S(1)} collective-permute-done((f32[256,512]{1,0:T(8,128)S(1)}, f32[256,512]{1,0:T(8,128)S(1)}, u32[]{:S(2)}, u32[]{:S(2)}) %collective-permute-start.10) | collective-permute-done | bytes 524320 | tf_op jit(solution)/shard_map/ppermute | solution.py:232
  48.6 2.1 %collective-permute-start.11 = (f32[256,512]{1,0:T(8,128)S(1)}, f32[256,512]{1,0:T(8,128)S(1)}, u32[]{:S(2)}, u32[]{:S(2)}) collective-permute-start(f32[256,512]{1,0:T(8,128)S(1)} %shard_map.50.refs_3_), channel_id=1, source_target_pairs={{0,4},{4,0},{1,5},{5,1},{2,6},{6,2},{3,7},{7,3},{8,12},{12,8},{9,1... | collective-permute-start | bytes 1572872 | tf_op jit(solution)/shard_map/ppermute | solution.py:232
  51.1 3.1 %collective-permute-start.14 = (f32[256,512]{1,0:T(8,128)S(1)}, f32[256,512]{1,0:T(8,128)S(1)}, u32[]{:S(2)}, u32[]{:S(2)}) collective-permute-start(f32[256,512]{1,0:T(8,128)S(1)} %shard_map.50.refs_3_), channel_id=1, source_target_pairs={{0,56},{8,0},{16,8},{24,16},{32,24},{40,32},{48,40},{56,48},{1,57}... | collective-permute-start | bytes 1572872 | tf_op jit(solution)/shard_map/ppermute | solution.py:227
  54.2 1.6 %collective-permute-start.5 = (f32[256,512]{1,0:T(8,128)S(1)}, f32[256,512]{1,0:T(8,128)S(1)}, u32[]{:S(2)}, u32[]{:S(2)}) collective-permute-start(f32[256,512]{1,0:T(8,128)S(1)} %collective-permute-done.4.refs_2_), channel_id=1, source_target_pairs={{0,4},{4,0},{1,5},{5,1},{2,6},{6,2},{3,7},{7,3},{8,12},{12,8},{9,1... | collective-permute-start | bytes 1572872 | tf_op jit(solution)/shard_map/ppermute | solution.py:232
  55.8 5.5 %shard_map.51.refs_2_.refs_5_ = f32[512,512]{1,0:T(8,128)} custom-call(s32[3]{0:T(128)} %pad_add_fusion.refs_0_, f32[512,4096]{1,0:T(8,128)} %refs_1_.11, f32[256,512]{1,0:T(8,128)} %copy-done.20, f32[256,512]{1,0:T(8,128)} %copy-done.6, f32[256,512]{1,0:T(8,128)} %copy-done.3, f32[512,512]{1,0:T(8,128)} %shard_map.49.refs_2_.refs_5_), custom_call_target="tpu_custom_call" | custom-call | flops 1207959552 | tf_op jit(solution)/shard_map/pallas_call | solution.py:105
  62.6 3.5 %collective-permute-start.12 = (f32[256,512]{1,0:T(8,128)S(1)}, f32[256,512]{1,0:T(8,128)S(1)}, u32[]{:S(2)}, u32[]{:S(2)}) collective-permute-start(f32[256,512]{1,0:T(8,128)S(1)} %shard_map.52.refs_4_), channel_id=1, source_target_pairs={{0,56},{8,0},{16,8},{24,16},{32,24},{40,32},{48,40},{56,48},{1,57}... | collective-permute-start | bytes 1572872 | tf_op jit(solution)/shard_map/ppermute | solution.py:227
  66.1 1.7 %collective-permute-start.16 = (f32[256,512]{1,0:T(8,128)S(1)}, f32[256,512]{1,0:T(8,128)S(1)}, u32[]{:S(2)}, u32[]{:S(2)}) collective-permute-start(f32[256,512]{1,0:T(8,128)S(1)} %copy-done.17), channel_id=1, source_target_pairs={{0,4},{4,0},{1,5},{5,1},{2,6},{6,2},{3,7},{7,3},{8,12},{12,8},{9,1... | collective-permute-start | bytes 1572872 | tf_op jit(solution)/shard_map/ppermute | solution.py:232
  67.8 4.8 %collective-permute-done.5.refs_1_.refs_4_ = f32[256,512]{1,0:T(8,128)S(1)} collective-permute-done((f32[256,512]{1,0:T(8,128)S(1)}, f32[256,512]{1,0:T(8,128)S(1)}, u32[]{:S(2)}, u32[]{:S(2)}) %collective-permute-start.5) | collective-permute-done | bytes 524320 | tf_op jit(solution)/shard_map/ppermute | solution.py:232
  73.5 5.5 %shard_map.53.refs_2_.refs_5_ = f32[512,512]{1,0:T(8,128)} custom-call(s32[3]{0:T(128)} %pad_add_fusion.refs_0_, f32[512,4096]{1,0:T(8,128)} %refs_1_.11, f32[256,512]{1,0:T(8,128)} %copy-done.19, f32[256,512]{1,0:T(8,128)} %copy-done.22, f32[256,512]{1,0:T(8,128)} %copy-done.8, f32[512,512]{1,0:T(8,128)} %shard_map.51.refs_2_.refs_5_), custom_call_target="tpu_custom_call" | custom-call | flops 1207959552 | tf_op jit(solution)/shard_map/pallas_call | solution.py:105
  80.3 3.5 %collective-permute-start.15 = (f32[256,512]{1,0:T(8,128)S(1)}, f32[256,512]{1,0:T(8,128)S(1)}, u32[]{:S(2)}, u32[]{:S(2)}) collective-permute-start(f32[256,512]{1,0:T(8,128)S(1)} %shard_map.54.refs_3_), channel_id=1, source_target_pairs={{0,56},{8,0},{16,8},{24,16},{32,24},{40,32},{48,40},{56,48},{1,57}... | collective-permute-start | bytes 1572872 | tf_op jit(solution)/shard_map/ppermute | solution.py:227
  84.6 5.5 %shard_map.55.refs_5_ = f32[512,512]{1,0:T(8,128)} custom-call(s32[3]{0:T(128)} %pad_add_fusion.refs_0_, f32[512,4096]{1,0:T(8,128)} %refs_1_.11, f32[256,512]{1,0:T(8,128)} %copy-done.24, f32[256,512]{1,0:T(8,128)} %copy-done.9, f32[256,512]{1,0:T(8,128)} %copy-done.4, f32[512,512]{1,0:T(8,128)} %shard_map.53.refs_2_.refs_5_), custom_call_target="tpu_custom_call" | custom-call | flops 1207959552 | tf_op jit(solution)/shard_map/pallas_call | solution.py:105
  91.9 5.6 %shard_map.56 = (f32[64,512]{1,0:T(8,128)}, f32[64,512]{1,0:T(8,128)}, f32[64,512]{1,0:T(8,128)}, f32[64,512]{1,0:T(8,128)}, f32[64,512]{1,0:T(8,128)}, /*index=...) custom-call(s32[3]{0:T(128)} %pad_add_fusion.refs_0_, f32[512,4096]{1,0:T(8,128)} %refs_1_.11, ...), custom_call_target="tpu_custom_call" | custom-call | flops 1207959552 | tf_op jit(solution)/shard_map/pallas_call | solution.py:105
  97.5 1.4 collective-permute-start.22
  98.9 2.6 %collective-permute-start.23 = (f32[64,512]{1,0:T(8,128)}, f32[64,512]{1,0:T(8,128)S(1)}, u32[]{:S(2)}, u32[]{:S(2)}) collective-permute-start(f32[64,512]{1,0:T(8,128)} %get-tuple-element.38), channel_id=1, source_target_pairs={{0,2},{1,3},{2,0},{3,1},{4,6},{5,7},{6,4},{7,5},{8,10},{9,11},{10,... | collective-permute-start | bytes 393224 | tf_op jit(solution)/shard_map/ppermute | solution.py:227
  103.8 1.6 %collective-permute-start.20 = (f32[64,512]{1,0:T(8,128)}, f32[64,512]{1,0:T(8,128)S(1)}, u32[]{:S(2)}, u32[]{:S(2)}) collective-permute-start(f32[64,512]{1,0:T(8,128)} %get-tuple-element.34), channel_id=1, source_target_pairs={{0,3},{1,0},{2,1},{3,2},{4,7},{5,4},{6,5},{7,6},{8,11},{9,8},{10,9... | collective-permute-start | bytes 393224 | tf_op jit(solution)/shard_map/ppermute | solution.py:227
  106.5 2.8 %collective-permute-start.25 = (f32[64,512]{1,0:T(8,128)S(1)}, f32[64,512]{1,0:T(8,128)S(1)}, u32[]{:S(2)}, u32[]{:S(2)}) collective-permute-start(f32[64,512]{1,0:T(8,128)S(1)} %shard_map.59.refs_0_), channel_id=1, source_target_pairs={{0,32},{8,40},{16,48},{24,56},{32,0},{40,8},{48,16},{56,24},{1,33}... | collective-permute-start | bytes 393224 | tf_op jit(solution)/shard_map/ppermute | solution.py:227
  111.9 2.5 %collective-permute-start.21 = (f32[64,512]{1,0:T(8,128)S(1)}, f32[64,512]{1,0:T(8,128)S(1)}, u32[]{:S(2)}, u32[]{:S(2)}) collective-permute-start(f32[64,512]{1,0:T(8,128)S(1)} %shard_map.57.refs_0_), channel_id=1, source_target_pairs={{0,32},{8,40},{16,48},{24,56},{32,0},{40,8},{48,16},{56,24},{1,33}... | collective-permute-start | bytes 393224 | tf_op jit(solution)/shard_map/ppermute | solution.py:227
  114.9 3.8 %collective-permute-start.31 = (f32[16,512]{1,0:T(8,128)S(1)}, f32[16,512]{1,0:T(8,128)S(1)}, u32[]{:S(2)}, u32[]{:S(2)}) collective-permute-start(f32[16,512]{1,0:T(8,128)S(1)} %get-tuple-element.46), channel_id=1, source_target_pairs={{0,130},{1,131},{2,128},{3,129},{64,194},{65,195},{66,192},{67,193... | collective-permute-start | bytes 98312 | tf_op jit(solution)/shard_map/ppermute | solution.py:300
  118.7 2.4 %collective-permute-done.21.refs_1_ = f32[64,512]{1,0:T(8,128)S(1)} collective-permute-done((f32[64,512]{1,0:T(8,128)S(1)}, f32[64,512]{1,0:T(8,128)S(1)}, u32[]{:S(2)}, u32[]{:S(2)}) %collective-permute-start.21) | collective-permute-done | bytes 131104 | tf_op jit(solution)/shard_map/ppermute | solution.py:227
  121.9 10.5 %collective-permute-start.32 = (f32[16,512]{1,0:T(8,128)S(1)}, f32[16,512]{1,0:T(8,128)S(1)}, u32[]{:S(2)}, u32[]{:S(2)}) collective-permute-start(f32[16,512]{1,0:T(8,128)S(1)} %get-tuple-element.47), channel_id=1, source_target_pairs={{0,192},{1,193},{2,194},{3,195},{64,128},{65,129},{66,130},{67,131... | collective-permute-start | bytes 98312 | tf_op jit(solution)/shard_map/ppermute | solution.py:300
  133.0 3.7 %collective-permute-start.28 = (f32[16,512]{1,0:T(8,128)S(1)}, f32[16,512]{1,0:T(8,128)S(1)}, u32[]{:S(2)}, u32[]{:S(2)}) collective-permute-start(f32[16,512]{1,0:T(8,128)S(1)} %get-tuple-element.43), channel_id=1, source_target_pairs={{0,64},{1,65},{2,66},{3,67},{64,1},{65,0},{66,3},{67,2},{128,192},... | collective-permute-start | bytes 98312 | tf_op jit(solution)/shard_map/ppermute | solution.py:300
  137.9 3.6 %collective-permute-done.29.refs_7_ = f32[16,512]{1,0:T(8,128)S(1)} collective-permute-done((f32[16,512]{1,0:T(8,128)S(1)}, f32[16,512]{1,0:T(8,128)S(1)}, u32[]{:S(2)}, u32[]{:S(2)}) %collective-permute-start.29) | collective-permute-done | bytes 32800 | tf_op jit(solution)/shard_map/ppermute | solution.py:300
  (103 shorter events, 23.0 us)
Async XLA Ops:
  4.3 5.1 %collective-permute-start = (f32[256,128]{1,0:T(8,128)S(1)}, f32[256,128]{1,0:T(8,128)S(1)}, u32[]{:S(2)}, u32[]{:S(2)}) collective-permute-start(f32[256,128]{1,0:T(8,128)S(1)} %get-tuple-element.28), channel_id=1, source_target_pairs={{0,64},{64,0},{128,192},{192,128},{1,65},{65,1},{129,193},{193,129... | collective-permute-start | bytes 393224 | tf_op jit(solution)/shard_map/ppermute | solution.py:232
  7.6 5.1 %collective-permute-start.1 = (f32[256,128]{1,0:T(8,128)S(1)}, f32[256,128]{1,0:T(8,128)S(1)}, u32[]{:S(2)}, u32[]{:S(2)}) collective-permute-start(f32[256,128]{1,0:T(8,128)S(1)} %get-tuple-element.29), channel_id=1, source_target_pairs={{0,128},{64,192},{128,0},{192,64},{1,129},{65,193},{129,1},{193,65... | collective-permute-start | bytes 393224 | tf_op jit(solution)/shard_map/ppermute | solution.py:232
  7.6 8.0 %collective-permute-start.2 = (f32[256,128]{1,0:T(8,128)S(1)}, f32[256,128]{1,0:T(8,128)S(1)}, u32[]{:S(2)}, u32[]{:S(2)}) collective-permute-start(f32[256,128]{1,0:T(8,128)S(1)} %get-tuple-element.30), channel_id=1, source_target_pairs={{0,192},{64,128},{128,64},{192,0},{1,193},{65,129},{129,65},{193,1... | collective-permute-start | bytes 393224 | tf_op jit(solution)/shard_map/ppermute | solution.py:232
  15.7 14.9 %collective-permute-start.8 = (f32[256,512]{1,0:T(8,128)S(1)}, f32[256,512]{1,0:T(8,128)S(1)}, u32[]{:S(2)}, u32[]{:S(2)}) collective-permute-start(f32[256,512]{1,0:T(8,128)S(1)} %shard_map.47.refs_2_), channel_id=1, source_target_pairs={{0,4},{4,0},{1,5},{5,1},{2,6},{6,2},{3,7},{7,3},{8,12},{12,8},{9,1... | collective-permute-start | bytes 1572872 | tf_op jit(solution)/shard_map/ppermute | solution.py:232
  16.8 16.4 %collective-permute-start.7 = (f32[256,512]{1,0:T(8,128)S(1)}, f32[256,512]{1,0:T(8,128)S(1)}, u32[]{:S(2)}, u32[]{:S(2)}) collective-permute-start(f32[256,512]{1,0:T(8,128)S(1)} %shard_map.47.refs_2_), channel_id=1, source_target_pairs={{0,56},{8,0},{16,8},{24,16},{32,24},{40,32},{48,40},{56,48},{1,57}... | collective-permute-start | bytes 1572872 | tf_op jit(solution)/shard_map/ppermute | solution.py:227
  22.4 15.6 %collective-permute-start.3 = (f32[256,512]{1,0:T(8,128)S(1)}, f32[256,512]{1,0:T(8,128)S(1)}, u32[]{:S(2)}, u32[]{:S(2)}) collective-permute-start(f32[256,512]{1,0:T(8,128)S(1)} %shard_map.47.refs_2_), channel_id=1, source_target_pairs={{0,8},{8,16},{16,24},{24,32},{32,40},{40,48},{48,56},{56,0},{1,9},... | collective-permute-start | bytes 1572872 | tf_op jit(solution)/shard_map/ppermute | solution.py:227
  33.3 13.7 %collective-permute-start.10 = (f32[256,512]{1,0:T(8,128)S(1)}, f32[256,512]{1,0:T(8,128)S(1)}, u32[]{:S(2)}, u32[]{:S(2)}) collective-permute-start(f32[256,512]{1,0:T(8,128)S(1)} %shard_map.48.refs_4_), channel_id=1, source_target_pairs={{0,4},{4,0},{1,5},{5,1},{2,6},{6,2},{3,7},{7,3},{8,12},{12,8},{9,1... | collective-permute-start | bytes 1572872 | tf_op jit(solution)/shard_map/ppermute | solution.py:232
  33.6 13.7 %collective-permute-start.9 = (f32[256,512]{1,0:T(8,128)S(1)}, f32[256,512]{1,0:T(8,128)S(1)}, u32[]{:S(2)}, u32[]{:S(2)}) collective-permute-start(f32[256,512]{1,0:T(8,128)S(1)} %shard_map.48.refs_4_), channel_id=1, source_target_pairs={{0,56},{8,0},{16,8},{24,16},{32,24},{40,32},{48,40},{56,48},{1,57}... | collective-permute-start | bytes 1572872 | tf_op jit(solution)/shard_map/ppermute | solution.py:227
  38.0 13.0 %collective-permute-start.4 = (f32[256,512]{1,0:T(8,128)S(1)}, f32[256,512]{1,0:T(8,128)S(1)}, u32[]{:S(2)}, u32[]{:S(2)}) collective-permute-start(f32[256,512]{1,0:T(8,128)S(1)} %collective-permute-done.3.refs_3_), channel_id=1, source_target_pairs={{0,8},{8,16},{16,24},{24,32},{32,40},{40,48},{48,56},{56,0},{1,9},... | collective-permute-start | bytes 1572872 | tf_op jit(solution)/shard_map/ppermute | solution.py:227
  48.6 12.8 %collective-permute-start.11 = (f32[256,512]{1,0:T(8,128)S(1)}, f32[256,512]{1,0:T(8,128)S(1)}, u32[]{:S(2)}, u32[]{:S(2)}) collective-permute-start(f32[256,512]{1,0:T(8,128)S(1)} %shard_map.50.refs_3_), channel_id=1, source_target_pairs={{0,4},{4,0},{1,5},{5,1},{2,6},{6,2},{3,7},{7,3},{8,12},{12,8},{9,1... | collective-permute-start | bytes 1572872 | tf_op jit(solution)/shard_map/ppermute | solution.py:232
  51.1 16.7 %collective-permute-start.13 = (f32[256,512]{1,0:T(8,128)S(1)}, f32[256,512]{1,0:T(8,128)S(1)}, u32[]{:S(2)}, u32[]{:S(2)}) collective-permute-start(f32[256,512]{1,0:T(8,128)S(1)} %collective-permute-done.4.refs_2_), channel_id=1, source_target_pairs={{0,8},{8,16},{16,24},{24,32},{32,40},{40,48},{48,56},{56,0},{1,9},... | collective-permute-start | bytes 1572872 | tf_op jit(solution)/shard_map/ppermute | solution.py:227
  51.1 21.5 %collective-permute-start.14 = (f32[256,512]{1,0:T(8,128)S(1)}, f32[256,512]{1,0:T(8,128)S(1)}, u32[]{:S(2)}, u32[]{:S(2)}) collective-permute-start(f32[256,512]{1,0:T(8,128)S(1)} %shard_map.50.refs_3_), channel_id=1, source_target_pairs={{0,56},{8,0},{16,8},{24,16},{32,24},{40,32},{48,40},{56,48},{1,57}... | collective-permute-start | bytes 1572872 | tf_op jit(solution)/shard_map/ppermute | solution.py:227
  54.2 18.4 %collective-permute-start.5 = (f32[256,512]{1,0:T(8,128)S(1)}, f32[256,512]{1,0:T(8,128)S(1)}, u32[]{:S(2)}, u32[]{:S(2)}) collective-permute-start(f32[256,512]{1,0:T(8,128)S(1)} %collective-permute-done.4.refs_2_), channel_id=1, source_target_pairs={{0,4},{4,0},{1,5},{5,1},{2,6},{6,2},{3,7},{7,3},{8,12},{12,8},{9,1... | collective-permute-start | bytes 1572872 | tf_op jit(solution)/shard_map/ppermute | solution.py:232
  62.6 16.3 %collective-permute-start.12 = (f32[256,512]{1,0:T(8,128)S(1)}, f32[256,512]{1,0:T(8,128)S(1)}, u32[]{:S(2)}, u32[]{:S(2)}) collective-permute-start(f32[256,512]{1,0:T(8,128)S(1)} %shard_map.52.refs_4_), channel_id=1, source_target_pairs={{0,56},{8,0},{16,8},{24,16},{32,24},{40,32},{48,40},{56,48},{1,57}... | collective-permute-start | bytes 1572872 | tf_op jit(solution)/shard_map/ppermute | solution.py:227
  66.1 24.0 %collective-permute-start.16 = (f32[256,512]{1,0:T(8,128)S(1)}, f32[256,512]{1,0:T(8,128)S(1)}, u32[]{:S(2)}, u32[]{:S(2)}) collective-permute-start(f32[256,512]{1,0:T(8,128)S(1)} %copy-done.17), channel_id=1, source_target_pairs={{0,4},{4,0},{1,5},{5,1},{2,6},{6,2},{3,7},{7,3},{8,12},{12,8},{9,1... | collective-permute-start | bytes 1572872 | tf_op jit(solution)/shard_map/ppermute | solution.py:232
  67.8 15.9 %collective-permute-start.17 = (f32[256,512]{1,0:T(8,128)S(1)}, f32[256,512]{1,0:T(8,128)S(1)}, u32[]{:S(2)}, u32[]{:S(2)}) collective-permute-start(f32[256,512]{1,0:T(8,128)S(1)} %collective-permute-done.13.refs_2_), channel_id=1, source_target_pairs={{0,8},{8,16},{16,24},{24,32},{32,40},{40,48},{48,56},{56,0},{1,9},... | collective-permute-start | bytes 1572872 | tf_op jit(solution)/shard_map/ppermute | solution.py:227
  72.6 17.5 %collective-permute-start.6 = (f32[256,512]{1,0:T(8,128)S(1)}, f32[256,512]{1,0:T(8,128)S(1)}, u32[]{:S(2)}, u32[]{:S(2)}) collective-permute-start(f32[256,512]{1,0:T(8,128)S(1)} %collective-permute-done.5.refs_1_.refs_4_), channel_id=1, source_target_pairs={{0,8},{8,16},{16,24},{24,32},{32,40},{40,48},{48,56},{56,0},{1,9},... | collective-permute-start | bytes 1572872 | tf_op jit(solution)/shard_map/ppermute | solution.py:227
  80.3 9.9 %collective-permute-start.15 = (f32[256,512]{1,0:T(8,128)S(1)}, f32[256,512]{1,0:T(8,128)S(1)}, u32[]{:S(2)}, u32[]{:S(2)}) collective-permute-start(f32[256,512]{1,0:T(8,128)S(1)} %shard_map.54.refs_3_), channel_id=1, source_target_pairs={{0,56},{8,0},{16,8},{24,16},{32,24},{40,32},{48,40},{56,48},{1,57}... | collective-permute-start | bytes 1572872 | tf_op jit(solution)/shard_map/ppermute | solution.py:227
  97.5 6.3 %collective-permute-start.22 = (f32[64,512]{1,0:T(8,128)}, f32[64,512]{1,0:T(8,128)S(1)}, u32[]{:S(2)}, u32[]{:S(2)}) collective-permute-start(f32[64,512]{1,0:T(8,128)} %get-tuple-element.37), channel_id=1, source_target_pairs={{0,1},{1,2},{2,3},{3,0},{4,5},{5,6},{6,7},{7,4},{8,9},{9,10},{10,1... | collective-permute-start | bytes 393224 | tf_op jit(solution)/shard_map/ppermute | solution.py:227
  98.9 6.6 %collective-permute-start.23 = (f32[64,512]{1,0:T(8,128)}, f32[64,512]{1,0:T(8,128)S(1)}, u32[]{:S(2)}, u32[]{:S(2)}) collective-permute-start(f32[64,512]{1,0:T(8,128)} %get-tuple-element.38), channel_id=1, source_target_pairs={{0,2},{1,3},{2,0},{3,1},{4,6},{5,7},{6,4},{7,5},{8,10},{9,11},{10,... | collective-permute-start | bytes 393224 | tf_op jit(solution)/shard_map/ppermute | solution.py:227
  102.6 7.5 %collective-permute-start.18 = (f32[64,512]{1,0:T(8,128)}, f32[64,512]{1,0:T(8,128)S(1)}, u32[]{:S(2)}, u32[]{:S(2)}) collective-permute-start(f32[64,512]{1,0:T(8,128)} %get-tuple-element.32), channel_id=1, source_target_pairs={{0,1},{1,2},{2,3},{3,0},{4,5},{5,6},{6,7},{7,4},{8,9},{9,10},{10,1... | collective-permute-start | bytes 393224 | tf_op jit(solution)/shard_map/ppermute | solution.py:227
  103.0 7.1 %collective-permute-start.19 = (f32[64,512]{1,0:T(8,128)}, f32[64,512]{1,0:T(8,128)S(1)}, u32[]{:S(2)}, u32[]{:S(2)}) collective-permute-start(f32[64,512]{1,0:T(8,128)} %get-tuple-element.33), channel_id=1, source_target_pairs={{0,2},{1,3},{2,0},{3,1},{4,6},{5,7},{6,4},{7,5},{8,10},{9,11},{10,... | collective-permute-start | bytes 393224 | tf_op jit(solution)/shard_map/ppermute | solution.py:227
  103.8 7.2 %collective-permute-start.20 = (f32[64,512]{1,0:T(8,128)}, f32[64,512]{1,0:T(8,128)S(1)}, u32[]{:S(2)}, u32[]{:S(2)}) collective-permute-start(f32[64,512]{1,0:T(8,128)} %get-tuple-element.34), channel_id=1, source_target_pairs={{0,3},{1,0},{2,1},{3,2},{4,7},{5,4},{6,5},{7,6},{8,11},{9,8},{10,9... | collective-permute-start | bytes 393224 | tf_op jit(solution)/shard_map/ppermute | solution.py:227
  106.5 8.0 %collective-permute-start.25 = (f32[64,512]{1,0:T(8,128)S(1)}, f32[64,512]{1,0:T(8,128)S(1)}, u32[]{:S(2)}, u32[]{:S(2)}) collective-permute-start(f32[64,512]{1,0:T(8,128)S(1)} %shard_map.59.refs_0_), channel_id=1, source_target_pairs={{0,32},{8,40},{16,48},{24,56},{32,0},{40,8},{48,16},{56,24},{1,33}... | collective-permute-start | bytes 393224 | tf_op jit(solution)/shard_map/ppermute | solution.py:227
  111.9 9.2 %collective-permute-start.21 = (f32[64,512]{1,0:T(8,128)S(1)}, f32[64,512]{1,0:T(8,128)S(1)}, u32[]{:S(2)}, u32[]{:S(2)}) collective-permute-start(f32[64,512]{1,0:T(8,128)S(1)} %shard_map.57.refs_0_), channel_id=1, source_target_pairs={{0,32},{8,40},{16,48},{24,56},{32,0},{40,8},{48,16},{56,24},{1,33}... | collective-permute-start | bytes 393224 | tf_op jit(solution)/shard_map/ppermute | solution.py:227
  114.5 18.5 %collective-permute-start.30 = (f32[16,512]{1,0:T(8,128)S(1)}, f32[16,512]{1,0:T(8,128)S(1)}, u32[]{:S(2)}, u32[]{:S(2)}) collective-permute-start(f32[16,512]{1,0:T(8,128)S(1)} %get-tuple-element.45), channel_id=1, source_target_pairs={{0,128},{1,129},{2,130},{3,131},{64,192},{65,193},{66,194},{67,195... | collective-permute-start | bytes 98312 | tf_op jit(solution)/shard_map/ppermute | solution.py:300
  114.9 21.8 %collective-permute-start.31 = (f32[16,512]{1,0:T(8,128)S(1)}, f32[16,512]{1,0:T(8,128)S(1)}, u32[]{:S(2)}, u32[]{:S(2)}) collective-permute-start(f32[16,512]{1,0:T(8,128)S(1)} %get-tuple-element.46), channel_id=1, source_target_pairs={{0,130},{1,131},{2,128},{3,129},{64,194},{65,195},{66,192},{67,193... | collective-permute-start | bytes 98312 | tf_op jit(solution)/shard_map/ppermute | solution.py:300
  121.2 11.3 %collective-permute-start.27 = (f32[8,512]{1,0:T(8,128)S(1)}, f32[8,512]{1,0:T(8,128)S(1)}, u32[]{:S(2)}, u32[]{:S(2)}) collective-permute-start(f32[8,512]{1,0:T(8,128)S(1)} %get-tuple-element.42), channel_id=1, source_target_pairs={{0,2},{1,3},{2,0},{3,1},{64,66},{65,67},{66,64},{67,65},{128,130},... | collective-permute-start | bytes 49160 | tf_op jit(solution)/shard_map/ppermute | solution.py:300
  121.9 15.6 %collective-permute-start.32 = (f32[16,512]{1,0:T(8,128)S(1)}, f32[16,512]{1,0:T(8,128)S(1)}, u32[]{:S(2)}, u32[]{:S(2)}) collective-permute-start(f32[16,512]{1,0:T(8,128)S(1)} %get-tuple-element.47), channel_id=1, source_target_pairs={{0,192},{1,193},{2,194},{3,195},{64,128},{65,129},{66,130},{67,131... | collective-permute-start | bytes 98312 | tf_op jit(solution)/shard_map/ppermute | solution.py:300
  132.5 5.4 %collective-permute-start.33 = (f32[16,512]{1,0:T(8,128)S(1)}, f32[16,512]{1,0:T(8,128)S(1)}, u32[]{:S(2)}, u32[]{:S(2)}) collective-permute-start(f32[16,512]{1,0:T(8,128)S(1)} %get-tuple-element.48), channel_id=1, source_target_pairs={{0,194},{1,195},{2,192},{3,193},{64,130},{65,131},{66,128},{67,129... | collective-permute-start | bytes 98312 | tf_op jit(solution)/shard_map/ppermute | solution.py:300
  132.5 5.4 %collective-permute-start.26 = (f32[16,512]{1,0:T(8,128)S(1)}, f32[16,512]{1,0:T(8,128)S(1)}, u32[]{:S(2)}, u32[]{:S(2)}) collective-permute-start(f32[16,512]{1,0:T(8,128)S(1)} %get-tuple-element.41), channel_id=1, source_target_pairs={{0,1},{1,2},{2,3},{3,0},{64,65},{65,66},{66,67},{67,64},{128,129},... | collective-permute-start | bytes 98312 | tf_op jit(solution)/shard_map/ppermute | solution.py:300
  133.0 4.9 %collective-permute-start.28 = (f32[16,512]{1,0:T(8,128)S(1)}, f32[16,512]{1,0:T(8,128)S(1)}, u32[]{:S(2)}, u32[]{:S(2)}) collective-permute-start(f32[16,512]{1,0:T(8,128)S(1)} %get-tuple-element.43), channel_id=1, source_target_pairs={{0,64},{1,65},{2,66},{3,67},{64,1},{65,0},{66,3},{67,2},{128,192},... | collective-permute-start | bytes 98312 | tf_op jit(solution)/shard_map/ppermute | solution.py:300
  (27 other events, 175.1 us)
where the time goes:
time: 143 us
  starting transfers between devices  65.1 us (46%)
  waiting for transfers between devices  33.2 us (23%)
  Pallas kernels  31.9 us (22%)
  local copies, waits for them, and re-layouts  11.6 us (8%)
    ppermute x18, starting transfers between devices, moved_along(): return lax.ppermute(value, axis, [(k, (k + step) % n) for k in range(n)])  32.7 us
    pallas_call x16, Pallas kernels, call(): pl.pallas_call(without_after, out_shape=out, in_specs=[pl.BlockSpec(memor...  31.9 us
    ppermute x8, waiting for transfers between devices, flipped(): return lax.ppermute(value, axes, [(k, k ^ mask) for k in range(n)])  21.6 us
    ppermute x8, starting transfers between devices, shards(): lax.ppermute(value, GROUP, perm)  20.6 us
    ppermute x8, starting transfers between devices, flipped(): return lax.ppermute(value, axes, [(k, k ^ mask) for k in range(n)])  11.9 us
    unnamed x50, local copies, waits for them, and re-layouts  11.6 us
    ppermute x18, waiting for transfers between devices, moved_along(): return lax.ppermute(value, axis, [(k, (k + step) % n) for k in range(n)])  7.61 us
    ppermute x8, waiting for transfers between devices, shards(): lax.ppermute(value, GROUP, perm)  4.01 us
  transfers between devices with their start and end apart: 34, of which 15 were waited for; matrix products, arithmetic and copies ran while one was open for 0% of the time, Pallas kernels for 16%

commit v1 on v0

--- a/solution.py
+++ b/solution.py
@@ -11,7 +11,7 @@
 O = 64
 GROUP = ("xl", "c", "y")
 F32, BF16 = jnp.float32, jnp.bfloat16
-VMEM_PRODUCT = 57 * 2**20
+VMEM_PRODUCT = 50 * 2**20
 
 
 def quad_partners(o, a, p):
@@ -113,11 +113,15 @@
     )(*args, *after)
 
 
-def in_step(value, after):
-    def body(source, target):
-        target[...] = source[...]
-
-    return call(body, [jax.ShapeDtypeStruct(value.shape, value.dtype)], value, after=after)[0]
+def in_step(turns, *arrays, after=()):
+    count = len(arrays)
+
+    def body(*refs):
+        refs = refs[len(turns):]
+        for source, target in zip(refs[:count], refs[count:]):
+            target[...] = source[...]
+
+    return call(body, [jax.ShapeDtypeStruct(a.shape, a.dtype) for a in arrays], *turns, *arrays, after=after)
 
 
 def f32(*shape):
@@ -157,6 +161,9 @@
     blocks = [refs.pop(0) for _ in places]
     before = refs.pop(0) if has_total else None
     outs = [refs.pop(0) for _ in range(8 if last else 1)]
+    if not last:
+        turn = refs.pop(0)
+        turn[...] = jnp.zeros_like(turn)
     held, sems, a_parts, b_parts, turned = refs
     depth, width = blocks[0].shape
     copies = []
@@ -265,7 +272,7 @@
     def product(held, places, total, last):
         n = len(places)
         args = (at, integrals, *[held[p] for p in places]) + ((total,) if total is not None else ())
-        out = [f32(64, 512)] * 8 if last else [f32(512, 512)]
+        out = [f32(64, 512)] * 8 if last else [f32(512, 512), f32(8, 128)]
         return call(functools.partial(product_body, places, total is not None, last), out, *args, smem=(0,), anywhere=(1,),
                     scratch=[pltpu.VMEM((n, 512, k), F32), pltpu.SemaphoreType.DMA((n,)), pltpu.VMEM((512, 3 * n * k), BF16),
                              pltpu.VMEM((3 * n * k, 512), BF16), pltpu.VMEM((512, 512), F32)],
@@ -273,24 +280,24 @@
 
     held = {(0, 0): unique}
     places, total = [(0, 0)], None
-    ready = ()
+    turns, last = (), ()
     for step in range(5):
-        down = STEPS[step][1]
         if step:
-            held[down] = in_step(held[down], ready)
-        arrived = gather_step(held, step)
-        ready = (held[arrived[2]],)
+            needed = list(dict.fromkeys(STEPS[step]))
+            others = [held[p] for p in last if p not in needed]
+            held.update(zip(needed, in_step(turns, *[held[p] for p in needed], after=others)))
+        last = gather_step(held, step)
         if step:
-            (total,) = product(held, tuple(places), total, False)
-            ready += (total,)
+            total, turn = product(held, tuple(places), total, False)
+            turns = (turn,)
             places = []
-        places += arrived
+        places += last
     total = product(held, tuple(places), total, True)
 
     perms = send_perms()
     pairs, arrived = [], []
     for n, pieces in enumerate((total[:4], total[4:])):
-        moved = [moved_along(pieces[r], "y", r) for r in (1, 2, 3)]
+        moved = [moved_along(pieces[r], "y", r) for r in (1, 3, 2)]
         (mine,) = call(sum_body, [f32(64, 512)], pieces[0], *moved)
         lots = perms[4 * n:4 * n + 4]
         cuts = [(slots[0] - 64 * n, len(slots)) for slots, _ in lots]

time: 143 us -> 134 us (0.937)
  waiting for transfers between devices: 33.2 us -> 46.9 us
  local copies, waits for them, and re-layouts: 11.6 us -> 1.98 us
  Pallas kernels: 31.9 us -> 22.8 us
  starting transfers between devices: 65.1 us -> 61.6 us
    ppermute x18, waiting for transfers between devices: 7.61 us -> 20.3 us  [moved_along(): return lax.ppermute(value, axis, [(k, (k + step) % n) for k in range(n)])]
    unnamed x50 -> x6, local copies, waits for them, and re-layouts: 11.6 us -> 1.98 us
    pallas_call x16, Pallas kernels: 31.9 us -> 22.8 us  [call(): pl.pallas_call(without_after, out_shape=out, in_specs=[pl.BlockSpec(memor...]
    ppermute x18, starting transfers between devices: 32.7 us -> 30 us  [moved_along(): return lax.ppermute(value, axis, [(k, (k + step) % n) for k in range(n)])]
  transfers between devices with their start and end apart: 34 -> 34, of which waited for: 15 -> 18; matrix products, arithmetic and copies ran while one was open for 0% -> 0% of each run, Pallas kernels for 16% -> 11%
where the time goes in v1:
time: 134 us
  starting transfers between devices  61.6 us (46%)
  waiting for transfers between devices  46.9 us (35%)
  Pallas kernels  22.8 us (17%)
  local copies, waits for them, and re-layouts  1.98 us (1%)
    ppermute x18, starting transfers between devices, moved_along(): return lax.ppermute(value, axis, [(k, (k + step) % n) for k in range(n)])  30 us
    pallas_call x16, Pallas kernels, call(): pl.pallas_call(without_after, out_shape=out, in_specs=[pl.BlockSpec(memor...  22.8 us
    ppermute x8, waiting for transfers between devices, flipped(): return lax.ppermute(value, axes, [(k, k ^ mask) for k in range(n)])  22.5 us
    ppermute x18, waiting for transfers between devices, moved_along(): return lax.ppermute(value, axis, [(k, (k + step) % n) for k in range(n)])  20.3 us
    ppermute x8, starting transfers between devices, shards(): lax.ppermute(value, GROUP, perm)  19.6 us
    ppermute x8, starting transfers between devices, flipped(): return lax.ppermute(value, axes, [(k, k ^ mask) for k in range(n)])  12 us
    ppermute x8, waiting for transfers between devices, shards(): lax.ppermute(value, GROUP, perm)  4.14 us
  transfers between devices with their start and end apart: 34, of which 18 were waited for; matrix products, arithmetic and copies ran while one was open for 0% of the time, Pallas kernels for 11%

profile of v1, /device:TPU:1, one launch (start us, length us, event | category | flops | bytes accessed | tf_op | source)
XLA Modules:
  0.0 133.6 jit_solution(7121060373406004866)
XLA Ops:
  2.0 2.3 %shard_map.46 = (f32[256,512]{1,0:T(8,128)S(1)}, f32[256,128]{1,0:T(8,128)S(1)}, f32[256,128]{1,0:T(8,128)S(1)}, f32[256,128]{1,0:T(8,128)S(1)}) custom-call(s32[1]{0:T(128)} %bitcast.4.refs_0_, s32[4,2,896]{2,1,0:T(2,128)S(1)} %copy-done.2, f32[256,1024]{1,0:T(8,128)S(1)} %copy-done), custom_call_target="tpu_custom_call" | custom-call | tf_op jit(solution)/shard_map/pallas_call | solution.py:105
  4.3 3.3 %collective-permute-start = (f32[256,128]{1,0:T(8,128)S(1)}, f32[256,128]{1,0:T(8,128)S(1)}, u32[]{:S(2)}, u32[]{:S(2)}) collective-permute-start(f32[256,128]{1,0:T(8,128)S(1)} %get-tuple-element.45), channel_id=1, source_target_pairs={{0,64},{64,0},{128,192},{192,128},{1,65},{65,1},{129,193},{193,129... | collective-permute-start | bytes 393224 | tf_op jit(solution)/shard_map/ppermute | solution.py:239
  9.4 3.3 %collective-permute-done.1.refs_2_ = f32[256,128]{1,0:T(8,128)S(1)} collective-permute-done((f32[256,128]{1,0:T(8,128)S(1)}, f32[256,128]{1,0:T(8,128)S(1)}, u32[]{:S(2)}, u32[]{:S(2)}) %collective-permute-start.1) | collective-permute-done | bytes 131104 | tf_op jit(solution)/shard_map/ppermute | solution.py:239
  12.7 3.0 %collective-permute-done.2.refs_3_ = f32[256,128]{1,0:T(8,128)S(1)} collective-permute-done((f32[256,128]{1,0:T(8,128)S(1)}, f32[256,128]{1,0:T(8,128)S(1)}, u32[]{:S(2)}, u32[]{:S(2)}) %collective-permute-start.2) | collective-permute-done | bytes 131104 | tf_op jit(solution)/shard_map/ppermute | solution.py:239
  16.8 5.6 %collective-permute-start.4 = (f32[256,512]{1,0:T(8,128)S(1)}, f32[256,512]{1,0:T(8,128)S(1)}, u32[]{:S(2)}, u32[]{:S(2)}) collective-permute-start(f32[256,512]{1,0:T(8,128)S(1)} %shard_map.47.refs_2_), channel_id=1, source_target_pairs={{0,56},{8,0},{16,8},{24,16},{32,24},{40,32},{48,40},{56,48},{1,57}... | collective-permute-start | bytes 1572872 | tf_op jit(solution)/shard_map/ppermute | solution.py:234
  22.4 8.2 %collective-permute-done.5.refs_2_.refs_5_ = f32[256,512]{1,0:T(8,128)S(1)} collective-permute-done((f32[256,512]{1,0:T(8,128)S(1)}, f32[256,512]{1,0:T(8,128)S(1)}, u32[]{:S(2)}, u32[]{:S(2)}) %collective-permute-start.5) | collective-permute-done | bytes 524320 | tf_op jit(solution)/shard_map/ppermute | solution.py:239
  30.6 2.6 %collective-permute-done.4.refs_1_ = f32[256,512]{1,0:T(8,128)S(1)} collective-permute-done((f32[256,512]{1,0:T(8,128)S(1)}, f32[256,512]{1,0:T(8,128)S(1)}, u32[]{:S(2)}, u32[]{:S(2)}) %collective-permute-start.4) | collective-permute-done | bytes 524320 | tf_op jit(solution)/shard_map/ppermute | solution.py:234
  33.2 3.1 %collective-permute-done.3.refs_0_ = f32[256,512]{1,0:T(8,128)S(1)} collective-permute-done((f32[256,512]{1,0:T(8,128)S(1)}, f32[256,512]{1,0:T(8,128)S(1)}, u32[]{:S(2)}, u32[]{:S(2)}) %collective-permute-start.3) | collective-permute-done | bytes 524320 | tf_op jit(solution)/shard_map/ppermute | solution.py:234
  37.4 2.7 %collective-permute-start.7 = (f32[256,512]{1,0:T(8,128)}, f32[256,512]{1,0:T(8,128)S(1)}, u32[]{:S(2)}, u32[]{:S(2)}) collective-permute-start(f32[256,512]{1,0:T(8,128)} %get-tuple-element.49.refs_4_), channel_id=1, source_target_pairs={{0,56},{8,0},{16,8},{24,16},{32,24},{40,32},{48,40},{56,48},{1,57}... | collective-permute-start | bytes 1572872 | tf_op jit(solution)/shard_map/ppermute | solution.py:234
  40.1 4.4 %shard_map.49 = (f32[512,512]{1,0:T(8,128)S(1)}, f32[8,128]{1,0:T(8,128)S(1)}) custom-call(s32[3]{0:T(128)S(1)} %pad_add_fusion.refs_0_, f32[512,4096]{1,0:T(8,128)} %refs_1_.11, f32[256,512]{1,0:T(8,128)S(1)} %shard_map.47.refs_2_, f32[256,512]{1,0:T(8,128)S(1)} %get-tuple-element.48.refs_3_, f32[256,512]{1,0:T(8,128)} %get-tuple-element.49.refs_4_, ...), custom_call_target="tpu_custom_call" | custom-call | flops 1610612736 | tf_op jit(solution)/shard_map/pallas_call | solution.py:105
  44.6 5.6 %collective-permute-done.6.refs_1_ = f32[256,512]{1,0:T(8,128)S(1)} collective-permute-done((f32[256,512]{1,0:T(8,128)S(1)}, f32[256,512]{1,0:T(8,128)S(1)}, u32[]{:S(2)}, u32[]{:S(2)}) %collective-permute-start.6) | collective-permute-done | bytes 524320 | tf_op jit(solution)/shard_map/ppermute | solution.py:234
  50.8 2.7 %collective-permute-start.11 = (f32[256,512]{1,0:T(8,128)S(1)}, f32[256,512]{1,0:T(8,128)S(1)}, u32[]{:S(2)}, u32[]{:S(2)}) collective-permute-start(f32[256,512]{1,0:T(8,128)S(1)} %get-tuple-element.52.refs_3_), channel_id=1, source_target_pairs={{0,56},{8,0},{16,8},{24,16},{32,24},{40,32},{48,40},{56,48},{1,57}... | collective-permute-start | bytes 1572872 | tf_op jit(solution)/shard_map/ppermute | solution.py:234
  53.5 2.2 %collective-permute-start.10 = (f32[256,512]{1,0:T(8,128)S(1)}, f32[256,512]{1,0:T(8,128)S(1)}, u32[]{:S(2)}, u32[]{:S(2)}) collective-permute-start(f32[256,512]{1,0:T(8,128)S(1)} %get-tuple-element.52.refs_3_), channel_id=1, source_target_pairs={{0,4},{4,0},{1,5},{5,1},{2,6},{6,2},{3,7},{7,3},{8,12},{12,8},{9,1... | collective-permute-start | bytes 1572872 | tf_op jit(solution)/shard_map/ppermute | solution.py:239
  55.7 3.3 %shard_map.51 = (f32[512,512]{1,0:T(8,128)S(1)}, f32[8,128]{1,0:T(8,128)S(1)}) custom-call(s32[3]{0:T(128)S(1)} %pad_add_fusion.refs_0_, f32[512,4096]{1,0:T(8,128)} %refs_1_.11, f32[256,512]{1,0:T(8,128)S(1)} %get-tuple-element.51.refs_2_.refs_3_, f32[256,512]{1,0:T(8,128)S(1)} %get-tuple-element.52.refs_3_, ...), custom_call_target="tpu_custom_call" | custom-call | flops 1207959552 | tf_op jit(solution)/shard_map/pallas_call | solution.py:105
  59.0 3.8 %collective-permute-done.9.refs_1_ = f32[256,512]{1,0:T(8,128)S(1)} collective-permute-done((f32[256,512]{1,0:T(8,128)S(1)}, f32[256,512]{1,0:T(8,128)S(1)}, u32[]{:S(2)}, u32[]{:S(2)}) %collective-permute-start.9) | collective-permute-done | bytes 524320 | tf_op jit(solution)/shard_map/ppermute | solution.py:234
  62.8 2.4 %collective-permute-done.10.refs_2_ = f32[256,512]{1,0:T(8,128)S(1)} collective-permute-done((f32[256,512]{1,0:T(8,128)S(1)}, f32[256,512]{1,0:T(8,128)S(1)}, u32[]{:S(2)}, u32[]{:S(2)}) %collective-permute-start.10) | collective-permute-done | bytes 524320 | tf_op jit(solution)/shard_map/ppermute | solution.py:239
  65.3 2.0 %collective-permute-start.12 = (f32[256,512]{1,0:T(8,128)S(1)}, f32[256,512]{1,0:T(8,128)S(1)}, u32[]{:S(2)}, u32[]{:S(2)}) collective-permute-start(f32[256,512]{1,0:T(8,128)S(1)} %get-tuple-element.59), channel_id=1, source_target_pairs={{0,4},{4,0},{1,5},{5,1},{2,6},{6,2},{3,7},{7,3},{8,12},{12,8},{9,1... | collective-permute-start | bytes 1572872 | tf_op jit(solution)/shard_map/ppermute | solution.py:239
  67.4 2.7 %collective-permute-start.13 = (f32[256,512]{1,0:T(8,128)S(1)}, f32[256,512]{1,0:T(8,128)S(1)}, u32[]{:S(2)}, u32[]{:S(2)}) collective-permute-start(f32[256,512]{1,0:T(8,128)S(1)} %get-tuple-element.56.refs_4_), channel_id=1, source_target_pairs={{0,56},{8,0},{16,8},{24,16},{32,24},{40,32},{48,40},{56,48},{1,57}... | collective-permute-start | bytes 1572872 | tf_op jit(solution)/shard_map/ppermute | solution.py:234
  70.0 3.3 %shard_map.53 = (f32[512,512]{1,0:T(8,128)S(1)}, f32[8,128]{1,0:T(8,128)S(1)}) custom-call(s32[3]{0:T(128)S(1)} %pad_add_fusion.refs_0_, f32[512,4096]{1,0:T(8,128)} %refs_1_.11, f32[256,512]{1,0:T(8,128)S(1)} %get-tuple-element.55.refs_2_, f32[256,512]{1,0:T(8,128)S(1)} %collective-permute-done.11.refs_4_.refs_3_, ...), custom_call_target="tpu_custom_call" | custom-call | flops 1207959552 | tf_op jit(solution)/shard_map/pallas_call | solution.py:105
  73.4 2.9 %collective-permute-done.12.refs_1_ = f32[256,512]{1,0:T(8,128)S(1)} collective-permute-done((f32[256,512]{1,0:T(8,128)S(1)}, f32[256,512]{1,0:T(8,128)S(1)}, u32[]{:S(2)}, u32[]{:S(2)}) %collective-permute-start.12) | collective-permute-done | bytes 524320 | tf_op jit(solution)/shard_map/ppermute | solution.py:239
  78.9 2.7 %collective-permute-start.16 = (f32[256,512]{1,0:T(8,128)S(1)}, f32[256,512]{1,0:T(8,128)S(1)}, u32[]{:S(2)}, u32[]{:S(2)}) collective-permute-start(f32[256,512]{1,0:T(8,128)S(1)} %get-tuple-element.61.refs_3_), channel_id=1, source_target_pairs={{0,56},{8,0},{16,8},{24,16},{32,24},{40,32},{48,40},{56,48},{1,57}... | collective-permute-start | bytes 1572872 | tf_op jit(solution)/shard_map/ppermute | solution.py:234
  81.6 3.3 %shard_map.55 = (f32[512,512]{1,0:T(8,128)S(1)}, f32[8,128]{1,0:T(8,128)}) custom-call(s32[3]{0:T(128)S(1)} %pad_add_fusion.refs_0_, f32[512,4096]{1,0:T(8,128)} %refs_1_.11, f32[256,512]{1,0:T(8,128)S(1)} %collective-permute-done.14.refs_4_.refs_2_, f32[256,512]{1,0:T(8,128)S(1)} %get-tuple-element.61.refs_3_, f32[256,512]{1,0:T(8,128)S(1)} %get-tuple-element.60.refs_4_, ...), custom_call_target="tpu_custom_call" | custom-call | flops 1207959552 | tf_op jit(solution)/shard_map/pallas_call | solution.py:105
  84.9 2.2 %collective-permute-done.17.refs_4_ = f32[256,512]{1,0:T(8,128)S(1)} collective-permute-done((f32[256,512]{1,0:T(8,128)S(1)}, f32[256,512]{1,0:T(8,128)S(1)}, u32[]{:S(2)}, u32[]{:S(2)}) %collective-permute-start.17) | collective-permute-done | bytes 524320 | tf_op jit(solution)/shard_map/ppermute | solution.py:239
  88.4 3.5 %shard_map.56 = (f32[64,512]{1,0:T(8,128)S(1)}, f32[64,512]{1,0:T(8,128)S(1)}, f32[64,512]{1,0:T(8,128)S(1)}, f32[64,512]{1,0:T(8,128)S(1)}, f32[64,512]{1,0:T(8...) custom-call(s32[3]{0:T(128)S(1)} %pad_add_fusion.refs_0_, f32[512,4096]{1,0:T(8,128)} %refs_1_.11, ...), custom_call_target="tpu_custom_call" | custom-call | flops 1207959552 | tf_op jit(solution)/shard_map/pallas_call | solution.py:105
  96.8 2.3 %collective-permute-start.23 = (f32[64,512]{1,0:T(8,128)S(1)}, f32[64,512]{1,0:T(8,128)S(1)}, u32[]{:S(2)}, u32[]{:S(2)}) collective-permute-start(f32[64,512]{1,0:T(8,128)S(1)} %get-tuple-element.72), channel_id=1, source_target_pairs={{0,3},{1,0},{2,1},{3,2},{4,7},{5,4},{6,5},{7,6},{8,11},{9,8},{10,9... | collective-permute-start | bytes 393224 | tf_op jit(solution)/shard_map/ppermute | solution.py:234
  100.2 3.0 %collective-permute-start.21 = (f32[64,512]{1,0:T(8,128)S(1)}, f32[64,512]{1,0:T(8,128)S(1)}, u32[]{:S(2)}, u32[]{:S(2)}) collective-permute-start(f32[64,512]{1,0:T(8,128)S(1)} %shard_map.57.refs_0_), channel_id=1, source_target_pairs={{0,32},{8,40},{16,48},{24,56},{32,0},{40,8},{48,16},{56,24},{1,33}... | collective-permute-start | bytes 393224 | tf_op jit(solution)/shard_map/ppermute | solution.py:234
  103.2 1.9 %collective-permute-done.24.refs_3_ = f32[64,512]{1,0:T(8,128)S(1)} collective-permute-done((f32[64,512]{1,0:T(8,128)S(1)}, f32[64,512]{1,0:T(8,128)S(1)}, u32[]{:S(2)}, u32[]{:S(2)}) %collective-permute-start.24) | collective-permute-done | bytes 131104 | tf_op jit(solution)/shard_map/ppermute | solution.py:234
  105.2 3.4 %collective-permute-start.25 = (f32[64,512]{1,0:T(8,128)S(1)}, f32[64,512]{1,0:T(8,128)S(1)}, u32[]{:S(2)}, u32[]{:S(2)}) collective-permute-start(f32[64,512]{1,0:T(8,128)S(1)} %shard_map.59.refs_0_), channel_id=1, source_target_pairs={{0,32},{8,40},{16,48},{24,56},{32,0},{40,8},{48,16},{56,24},{1,33}... | collective-permute-start | bytes 393224 | tf_op jit(solution)/shard_map/ppermute | solution.py:234
  108.7 10.5 %collective-permute-start.28 = (f32[16,512]{1,0:T(8,128)S(1)}, f32[16,512]{1,0:T(8,128)S(1)}, u32[]{:S(2)}, u32[]{:S(2)}) collective-permute-start(f32[16,512]{1,0:T(8,128)S(1)} %get-tuple-element.77), channel_id=1, source_target_pairs={{0,64},{1,65},{2,66},{3,67},{64,1},{65,0},{66,3},{67,2},{128,192},... | collective-permute-start | bytes 98312 | tf_op jit(solution)/shard_map/ppermute | solution.py:307
  119.2 2.2 %collective-permute-start.27 = (f32[8,512]{1,0:T(8,128)S(1)}, f32[8,512]{1,0:T(8,128)S(1)}, u32[]{:S(2)}, u32[]{:S(2)}) collective-permute-start(f32[8,512]{1,0:T(8,128)S(1)} %get-tuple-element.76), channel_id=1, source_target_pairs={{0,2},{1,3},{2,0},{3,1},{64,66},{65,67},{66,64},{67,65},{128,130},... | collective-permute-start | bytes 49160 | tf_op jit(solution)/shard_map/ppermute | solution.py:307
  123.3 2.8 %collective-permute-start.31 = (f32[16,512]{1,0:T(8,128)S(1)}, f32[16,512]{1,0:T(8,128)S(1)}, u32[]{:S(2)}, u32[]{:S(2)}) collective-permute-start(f32[16,512]{1,0:T(8,128)S(1)} %get-tuple-element.80), channel_id=1, source_target_pairs={{0,130},{1,131},{2,128},{3,129},{64,194},{65,195},{66,192},{67,193... | collective-permute-start | bytes 98312 | tf_op jit(solution)/shard_map/ppermute | solution.py:307
  126.9 2.2 %collective-permute-start.33 = (f32[16,512]{1,0:T(8,128)S(1)}, f32[16,512]{1,0:T(8,128)S(1)}, u32[]{:S(2)}, u32[]{:S(2)}) collective-permute-start(f32[16,512]{1,0:T(8,128)S(1)} %get-tuple-element.82), channel_id=1, source_target_pairs={{0,194},{1,195},{2,192},{3,193},{64,130},{65,131},{66,128},{67,129... | collective-permute-start | bytes 98312 | tf_op jit(solution)/shard_map/ppermute | solution.py:307
  (59 shorter events, 24.1 us)
Async XLA Ops:
  4.3 5.1 %collective-permute-start = (f32[256,128]{1,0:T(8,128)S(1)}, f32[256,128]{1,0:T(8,128)S(1)}, u32[]{:S(2)}, u32[]{:S(2)}) collective-permute-start(f32[256,128]{1,0:T(8,128)S(1)} %get-tuple-element.45), channel_id=1, source_target_pairs={{0,64},{64,0},{128,192},{192,128},{1,65},{65,1},{129,193},{193,129... | collective-permute-start | bytes 393224 | tf_op jit(solution)/shard_map/ppermute | solution.py:239
  7.6 5.1 %collective-permute-start.1 = (f32[256,128]{1,0:T(8,128)S(1)}, f32[256,128]{1,0:T(8,128)S(1)}, u32[]{:S(2)}, u32[]{:S(2)}) collective-permute-start(f32[256,128]{1,0:T(8,128)S(1)} %get-tuple-element.46), channel_id=1, source_target_pairs={{0,128},{64,192},{128,0},{192,64},{1,129},{65,193},{129,1},{193,65... | collective-permute-start | bytes 393224 | tf_op jit(solution)/shard_map/ppermute | solution.py:239
  7.6 8.0 %collective-permute-start.2 = (f32[256,128]{1,0:T(8,128)S(1)}, f32[256,128]{1,0:T(8,128)S(1)}, u32[]{:S(2)}, u32[]{:S(2)}) collective-permute-start(f32[256,128]{1,0:T(8,128)S(1)} %get-tuple-element.47), channel_id=1, source_target_pairs={{0,192},{64,128},{128,64},{192,0},{1,193},{65,129},{129,65},{193,1... | collective-permute-start | bytes 393224 | tf_op jit(solution)/shard_map/ppermute | solution.py:239
  15.7 14.9 %collective-permute-start.5 = (f32[256,512]{1,0:T(8,128)S(1)}, f32[256,512]{1,0:T(8,128)S(1)}, u32[]{:S(2)}, u32[]{:S(2)}) collective-permute-start(f32[256,512]{1,0:T(8,128)S(1)} %shard_map.47.refs_2_), channel_id=1, source_target_pairs={{0,4},{4,0},{1,5},{5,1},{2,6},{6,2},{3,7},{7,3},{8,12},{12,8},{9,1... | collective-permute-start | bytes 1572872 | tf_op jit(solution)/shard_map/ppermute | solution.py:239
  16.8 16.4 %collective-permute-start.4 = (f32[256,512]{1,0:T(8,128)S(1)}, f32[256,512]{1,0:T(8,128)S(1)}, u32[]{:S(2)}, u32[]{:S(2)}) collective-permute-start(f32[256,512]{1,0:T(8,128)S(1)} %shard_map.47.refs_2_), channel_id=1, source_target_pairs={{0,56},{8,0},{16,8},{24,16},{32,24},{40,32},{48,40},{56,48},{1,57}... | collective-permute-start | bytes 1572872 | tf_op jit(solution)/shard_map/ppermute | solution.py:234
  22.4 13.9 %collective-permute-start.3 = (f32[256,512]{1,0:T(8,128)S(1)}, f32[256,512]{1,0:T(8,128)S(1)}, u32[]{:S(2)}, u32[]{:S(2)}) collective-permute-start(f32[256,512]{1,0:T(8,128)S(1)} %shard_map.47.refs_2_), channel_id=1, source_target_pairs={{0,8},{8,16},{16,24},{24,32},{32,40},{40,48},{48,56},{56,0},{1,9},... | collective-permute-start | bytes 1572872 | tf_op jit(solution)/shard_map/ppermute | solution.py:234
  37.2 13.0 %collective-permute-start.6 = (f32[256,512]{1,0:T(8,128)S(1)}, f32[256,512]{1,0:T(8,128)S(1)}, u32[]{:S(2)}, u32[]{:S(2)}) collective-permute-start(f32[256,512]{1,0:T(8,128)S(1)} %get-tuple-element.48.refs_3_), channel_id=1, source_target_pairs={{0,8},{8,16},{16,24},{24,32},{32,40},{40,48},{48,56},{56,0},{1,9},... | collective-permute-start | bytes 1572872 | tf_op jit(solution)/shard_map/ppermute | solution.py:234
  37.2 13.5 %collective-permute-start.8 = (f32[256,512]{1,0:T(8,128)}, f32[256,512]{1,0:T(8,128)S(1)}, u32[]{:S(2)}, u32[]{:S(2)}) collective-permute-start(f32[256,512]{1,0:T(8,128)} %get-tuple-element.49.refs_4_), channel_id=1, source_target_pairs={{0,4},{4,0},{1,5},{5,1},{2,6},{6,2},{3,7},{7,3},{8,12},{12,8},{9,1... | collective-permute-start | bytes 1572872 | tf_op jit(solution)/shard_map/ppermute | solution.py:239
  37.4 13.2 %collective-permute-start.7 = (f32[256,512]{1,0:T(8,128)}, f32[256,512]{1,0:T(8,128)S(1)}, u32[]{:S(2)}, u32[]{:S(2)}) collective-permute-start(f32[256,512]{1,0:T(8,128)} %get-tuple-element.49.refs_4_), channel_id=1, source_target_pairs={{0,56},{8,0},{16,8},{24,16},{32,24},{40,32},{48,40},{56,48},{1,57}... | collective-permute-start | bytes 1572872 | tf_op jit(solution)/shard_map/ppermute | solution.py:234
  50.7 12.1 %collective-permute-start.9 = (f32[256,512]{1,0:T(8,128)S(1)}, f32[256,512]{1,0:T(8,128)S(1)}, u32[]{:S(2)}, u32[]{:S(2)}) collective-permute-start(f32[256,512]{1,0:T(8,128)S(1)} %get-tuple-element.51.refs_2_.refs_3_), channel_id=1, source_target_pairs={{0,8},{8,16},{16,24},{24,32},{32,40},{40,48},{48,56},{56,0},{1,9},... | collective-permute-start | bytes 1572872 | tf_op jit(solution)/shard_map/ppermute | solution.py:234
  50.8 12.0 %collective-permute-start.11 = (f32[256,512]{1,0:T(8,128)S(1)}, f32[256,512]{1,0:T(8,128)S(1)}, u32[]{:S(2)}, u32[]{:S(2)}) collective-permute-start(f32[256,512]{1,0:T(8,128)S(1)} %get-tuple-element.52.refs_3_), channel_id=1, source_target_pairs={{0,56},{8,0},{16,8},{24,16},{32,24},{40,32},{48,40},{56,48},{1,57}... | collective-permute-start | bytes 1572872 | tf_op jit(solution)/shard_map/ppermute | solution.py:234
  53.5 11.8 %collective-permute-start.10 = (f32[256,512]{1,0:T(8,128)S(1)}, f32[256,512]{1,0:T(8,128)S(1)}, u32[]{:S(2)}, u32[]{:S(2)}) collective-permute-start(f32[256,512]{1,0:T(8,128)S(1)} %get-tuple-element.52.refs_3_), channel_id=1, source_target_pairs={{0,4},{4,0},{1,5},{5,1},{2,6},{6,2},{3,7},{7,3},{8,12},{12,8},{9,1... | collective-permute-start | bytes 1572872 | tf_op jit(solution)/shard_map/ppermute | solution.py:239
  65.3 10.9 %collective-permute-start.12 = (f32[256,512]{1,0:T(8,128)S(1)}, f32[256,512]{1,0:T(8,128)S(1)}, u32[]{:S(2)}, u32[]{:S(2)}) collective-permute-start(f32[256,512]{1,0:T(8,128)S(1)} %get-tuple-element.59), channel_id=1, source_target_pairs={{0,4},{4,0},{1,5},{5,1},{2,6},{6,2},{3,7},{7,3},{8,12},{12,8},{9,1... | collective-permute-start | bytes 1572872 | tf_op jit(solution)/shard_map/ppermute | solution.py:239
  67.3 10.0 %collective-permute-start.14 = (f32[256,512]{1,0:T(8,128)S(1)}, f32[256,512]{1,0:T(8,128)S(1)}, u32[]{:S(2)}, u32[]{:S(2)}) collective-permute-start(f32[256,512]{1,0:T(8,128)S(1)} %get-tuple-element.55.refs_2_), channel_id=1, source_target_pairs={{0,8},{8,16},{16,24},{24,32},{32,40},{40,48},{48,56},{56,0},{1,9},... | collective-permute-start | bytes 1572872 | tf_op jit(solution)/shard_map/ppermute | solution.py:234
  67.4 10.0 %collective-permute-start.13 = (f32[256,512]{1,0:T(8,128)S(1)}, f32[256,512]{1,0:T(8,128)S(1)}, u32[]{:S(2)}, u32[]{:S(2)}) collective-permute-start(f32[256,512]{1,0:T(8,128)S(1)} %get-tuple-element.56.refs_4_), channel_id=1, source_target_pairs={{0,56},{8,0},{16,8},{24,16},{32,24},{40,32},{48,40},{56,48},{1,57}... | collective-permute-start | bytes 1572872 | tf_op jit(solution)/shard_map/ppermute | solution.py:234
  77.5 9.6 %collective-permute-start.17 = (f32[256,512]{1,0:T(8,128)S(1)}, f32[256,512]{1,0:T(8,128)S(1)}, u32[]{:S(2)}, u32[]{:S(2)}) collective-permute-start(f32[256,512]{1,0:T(8,128)S(1)} %get-tuple-element.62), channel_id=1, source_target_pairs={{0,4},{4,0},{1,5},{5,1},{2,6},{6,2},{3,7},{7,3},{8,12},{12,8},{9,1... | collective-permute-start | bytes 1572872 | tf_op jit(solution)/shard_map/ppermute | solution.py:239
  78.9 9.5 %collective-permute-start.15 = (f32[256,512]{1,0:T(8,128)S(1)}, f32[256,512]{1,0:T(8,128)S(1)}, u32[]{:S(2)}, u32[]{:S(2)}) collective-permute-start(f32[256,512]{1,0:T(8,128)S(1)} %get-tuple-element.60.refs_4_), channel_id=1, source_target_pairs={{0,8},{8,16},{16,24},{24,32},{32,40},{40,48},{48,56},{56,0},{1,9},... | collective-permute-start | bytes 1572872 | tf_op jit(solution)/shard_map/ppermute | solution.py:234
  78.9 9.5 %collective-permute-start.16 = (f32[256,512]{1,0:T(8,128)S(1)}, f32[256,512]{1,0:T(8,128)S(1)}, u32[]{:S(2)}, u32[]{:S(2)}) collective-permute-start(f32[256,512]{1,0:T(8,128)S(1)} %get-tuple-element.61.refs_3_), channel_id=1, source_target_pairs={{0,56},{8,0},{16,8},{24,16},{32,24},{40,32},{48,40},{56,48},{1,57}... | collective-permute-start | bytes 1572872 | tf_op jit(solution)/shard_map/ppermute | solution.py:234
  92.0 7.1 %collective-permute-start.18 = (f32[64,512]{1,0:T(8,128)S(1)}, f32[64,512]{1,0:T(8,128)S(1)}, u32[]{:S(2)}, u32[]{:S(2)}) collective-permute-start(f32[64,512]{1,0:T(8,128)S(1)} %get-tuple-element.66), channel_id=1, source_target_pairs={{0,1},{1,2},{2,3},{3,0},{4,5},{5,6},{6,7},{7,4},{8,9},{9,10},{10,1... | collective-permute-start | bytes 393224 | tf_op jit(solution)/shard_map/ppermute | solution.py:234
  93.3 6.0 %collective-permute-start.19 = (f32[64,512]{1,0:T(8,128)S(1)}, f32[64,512]{1,0:T(8,128)S(1)}, u32[]{:S(2)}, u32[]{:S(2)}) collective-permute-start(f32[64,512]{1,0:T(8,128)S(1)} %get-tuple-element.67), channel_id=1, source_target_pairs={{0,3},{1,0},{2,1},{3,2},{4,7},{5,4},{6,5},{7,6},{8,11},{9,8},{10,9... | collective-permute-start | bytes 393224 | tf_op jit(solution)/shard_map/ppermute | solution.py:234
  94.9 5.3 %collective-permute-start.20 = (f32[64,512]{1,0:T(8,128)S(1)}, f32[64,512]{1,0:T(8,128)S(1)}, u32[]{:S(2)}, u32[]{:S(2)}) collective-permute-start(f32[64,512]{1,0:T(8,128)S(1)} %get-tuple-element.68), channel_id=1, source_target_pairs={{0,2},{1,3},{2,0},{3,1},{4,6},{5,7},{6,4},{7,5},{8,10},{9,11},{10,... | collective-permute-start | bytes 393224 | tf_op jit(solution)/shard_map/ppermute | solution.py:234
  96.4 6.8 %collective-permute-start.22 = (f32[64,512]{1,0:T(8,128)S(1)}, f32[64,512]{1,0:T(8,128)S(1)}, u32[]{:S(2)}, u32[]{:S(2)}) collective-permute-start(f32[64,512]{1,0:T(8,128)S(1)} %get-tuple-element.71), channel_id=1, source_target_pairs={{0,1},{1,2},{2,3},{3,0},{4,5},{5,6},{6,7},{7,4},{8,9},{9,10},{10,1... | collective-permute-start | bytes 393224 | tf_op jit(solution)/shard_map/ppermute | solution.py:234
  96.8 6.4 %collective-permute-start.23 = (f32[64,512]{1,0:T(8,128)S(1)}, f32[64,512]{1,0:T(8,128)S(1)}, u32[]{:S(2)}, u32[]{:S(2)}) collective-permute-start(f32[64,512]{1,0:T(8,128)S(1)} %get-tuple-element.72), channel_id=1, source_target_pairs={{0,3},{1,0},{2,1},{3,2},{4,7},{5,4},{6,5},{7,6},{8,11},{9,8},{10,9... | collective-permute-start | bytes 393224 | tf_op jit(solution)/shard_map/ppermute | solution.py:234
  99.1 6.0 %collective-permute-start.24 = (f32[64,512]{1,0:T(8,128)S(1)}, f32[64,512]{1,0:T(8,128)S(1)}, u32[]{:S(2)}, u32[]{:S(2)}) collective-permute-start(f32[64,512]{1,0:T(8,128)S(1)} %get-tuple-element.73), channel_id=1, source_target_pairs={{0,2},{1,3},{2,0},{3,1},{4,6},{5,7},{6,4},{7,5},{8,10},{9,11},{10,... | collective-permute-start | bytes 393224 | tf_op jit(solution)/shard_map/ppermute | solution.py:234
  100.2 8.3 %collective-permute-start.21 = (f32[64,512]{1,0:T(8,128)S(1)}, f32[64,512]{1,0:T(8,128)S(1)}, u32[]{:S(2)}, u32[]{:S(2)}) collective-permute-start(f32[64,512]{1,0:T(8,128)S(1)} %shard_map.57.refs_0_), channel_id=1, source_target_pairs={{0,32},{8,40},{16,48},{24,56},{32,0},{40,8},{48,16},{56,24},{1,33}... | collective-permute-start | bytes 393224 | tf_op jit(solution)/shard_map/ppermute | solution.py:234
  105.2 16.7 %collective-permute-start.25 = (f32[64,512]{1,0:T(8,128)S(1)}, f32[64,512]{1,0:T(8,128)S(1)}, u32[]{:S(2)}, u32[]{:S(2)}) collective-permute-start(f32[64,512]{1,0:T(8,128)S(1)} %shard_map.59.refs_0_), channel_id=1, source_target_pairs={{0,32},{8,40},{16,48},{24,56},{32,0},{40,8},{48,16},{56,24},{1,33}... | collective-permute-start | bytes 393224 | tf_op jit(solution)/shard_map/ppermute | solution.py:234
  108.6 17.5 %collective-permute-start.26 = (f32[16,512]{1,0:T(8,128)S(1)}, f32[16,512]{1,0:T(8,128)S(1)}, u32[]{:S(2)}, u32[]{:S(2)}) collective-permute-start(f32[16,512]{1,0:T(8,128)S(1)} %get-tuple-element.75), channel_id=1, source_target_pairs={{0,1},{1,2},{2,3},{3,0},{64,65},{65,66},{66,67},{67,64},{128,129},... | collective-permute-start | bytes 98312 | tf_op jit(solution)/shard_map/ppermute | solution.py:307
  108.7 18.2 %collective-permute-start.28 = (f32[16,512]{1,0:T(8,128)S(1)}, f32[16,512]{1,0:T(8,128)S(1)}, u32[]{:S(2)}, u32[]{:S(2)}) collective-permute-start(f32[16,512]{1,0:T(8,128)S(1)} %get-tuple-element.77), channel_id=1, source_target_pairs={{0,64},{1,65},{2,66},{3,67},{64,1},{65,0},{66,3},{67,2},{128,192},... | collective-permute-start | bytes 98312 | tf_op jit(solution)/shard_map/ppermute | solution.py:307
  121.4 7.7 %collective-permute-start.29 = (f32[16,512]{1,0:T(8,128)S(1)}, f32[16,512]{1,0:T(8,128)S(1)}, u32[]{:S(2)}, u32[]{:S(2)}) collective-permute-start(f32[16,512]{1,0:T(8,128)S(1)} %get-tuple-element.78), channel_id=1, source_target_pairs={{0,66},{1,67},{2,64},{3,65},{64,3},{65,2},{66,1},{67,0},{128,194},... | collective-permute-start | bytes 98312 | tf_op jit(solution)/shard_map/ppermute | solution.py:307
  121.9 7.2 %collective-permute-start.30 = (f32[16,512]{1,0:T(8,128)S(1)}, f32[16,512]{1,0:T(8,128)S(1)}, u32[]{:S(2)}, u32[]{:S(2)}) collective-permute-start(f32[16,512]{1,0:T(8,128)S(1)} %get-tuple-element.79), channel_id=1, source_target_pairs={{0,128},{1,129},{2,130},{3,131},{64,192},{65,193},{66,194},{67,195... | collective-permute-start | bytes 98312 | tf_op jit(solution)/shard_map/ppermute | solution.py:307
  123.3 5.8 %collective-permute-start.31 = (f32[16,512]{1,0:T(8,128)S(1)}, f32[16,512]{1,0:T(8,128)S(1)}, u32[]{:S(2)}, u32[]{:S(2)}) collective-permute-start(f32[16,512]{1,0:T(8,128)S(1)} %get-tuple-element.80), channel_id=1, source_target_pairs={{0,130},{1,131},{2,128},{3,129},{64,194},{65,195},{66,192},{67,193... | collective-permute-start | bytes 98312 | tf_op jit(solution)/shard_map/ppermute | solution.py:307
  126.9 5.5 %collective-permute-start.33 = (f32[16,512]{1,0:T(8,128)S(1)}, f32[16,512]{1,0:T(8,128)S(1)}, u32[]{:S(2)}, u32[]{:S(2)}) collective-permute-start(f32[16,512]{1,0:T(8,128)S(1)} %get-tuple-element.82), channel_id=1, source_target_pairs={{0,194},{1,195},{2,192},{3,193},{64,130},{65,131},{66,128},{67,129... | collective-permute-start | bytes 98312 | tf_op jit(solution)/shard_map/ppermute | solution.py:307
  (5 other events, 58.1 us)

commit v2 on v1

--- a/solution.py
+++ b/solution.py
@@ -223,7 +223,7 @@
     hot = jnp.where(row == table[0:1, :], table[1:2, :].astype(F32), 0.0).astype(BF16)
     turned = held[...].T
     acc = None
-    for part in parts_of(turned, 3):
+    for part in parts_of(turned, 2):
         term = jnp.dot(part, hot, preferred_element_type=F32)
         acc = term if acc is None else acc + term
     o_ref[...] = acc

time: 134 us -> 134 us (level)
  no operation moved by 1% of the time
where the time goes in v2:
time: 134 us
  starting transfers between devices  61.6 us (46%)
  waiting for transfers between devices  46.9 us (35%)
  Pallas kernels  22.7 us (17%)
  local copies, waits for them, and re-layouts  1.98 us (1%)
    ppermute x18, starting transfers between devices, moved_along(): return lax.ppermute(value, axis, [(k, (k + step) % n) for k in range(n)])  30 us
    pallas_call x16, Pallas kernels, call(): pl.pallas_call(without_after, out_shape=out, in_specs=[pl.BlockSpec(memor...  22.7 us
    ppermute x8, waiting for transfers between devices, flipped(): return lax.ppermute(value, axes, [(k, k ^ mask) for k in range(n)])  22.5 us
    ppermute x18, waiting for transfers between devices, moved_along(): return lax.ppermute(value, axis, [(k, (k + step) % n) for k in range(n)])  20.3 us
    ppermute x8, starting transfers between devices, shards(): lax.ppermute(value, GROUP, perm)  19.6 us
    ppermute x8, starting transfers between devices, flipped(): return lax.ppermute(value, axes, [(k, k ^ mask) for k in range(n)])  12 us
    ppermute x8, waiting for transfers between devices, shards(): lax.ppermute(value, GROUP, perm)  4.14 us
  transfers between devices with their start and end apart: 34, of which 18 were waited for; matrix products, arithmetic and copies ran while one was open for 0% of the time, Pallas kernels for 11%

profile of v2, /device:TPU:1, one launch (start us, length us, event | category | flops | bytes accessed | tf_op | source)
XLA Modules:
  0.0 133.5 jit_solution(1352729459362281444)
XLA Ops:
  2.0 2.3 %shard_map.46 = (f32[256,512]{1,0:T(8,128)S(1)}, f32[256,128]{1,0:T(8,128)S(1)}, f32[256,128]{1,0:T(8,128)S(1)}, f32[256,128]{1,0:T(8,128)S(1)}) custom-call(s32[1]{0:T(128)} %bitcast.4.refs_0_, s32[4,2,896]{2,1,0:T(2,128)S(1)} %copy-done.2, f32[256,1024]{1,0:T(8,128)S(1)} %copy-done), custom_call_target="tpu_custom_call" | custom-call | tf_op jit(solution)/shard_map/pallas_call | solution.py:105
  4.3 3.3 %collective-permute-start = (f32[256,128]{1,0:T(8,128)S(1)}, f32[256,128]{1,0:T(8,128)S(1)}, u32[]{:S(2)}, u32[]{:S(2)}) collective-permute-start(f32[256,128]{1,0:T(8,128)S(1)} %get-tuple-element.45), channel_id=1, source_target_pairs={{0,64},{64,0},{128,192},{192,128},{1,65},{65,1},{129,193},{193,129... | collective-permute-start | bytes 393224 | tf_op jit(solution)/shard_map/ppermute | solution.py:239
  9.4 3.3 %collective-permute-done.1.refs_2_ = f32[256,128]{1,0:T(8,128)S(1)} collective-permute-done((f32[256,128]{1,0:T(8,128)S(1)}, f32[256,128]{1,0:T(8,128)S(1)}, u32[]{:S(2)}, u32[]{:S(2)}) %collective-permute-start.1) | collective-permute-done | bytes 131104 | tf_op jit(solution)/shard_map/ppermute | solution.py:239
  12.7 3.0 %collective-permute-done.2.refs_3_ = f32[256,128]{1,0:T(8,128)S(1)} collective-permute-done((f32[256,128]{1,0:T(8,128)S(1)}, f32[256,128]{1,0:T(8,128)S(1)}, u32[]{:S(2)}, u32[]{:S(2)}) %collective-permute-start.2) | collective-permute-done | bytes 131104 | tf_op jit(solution)/shard_map/ppermute | solution.py:239
  16.8 5.6 %collective-permute-start.4 = (f32[256,512]{1,0:T(8,128)S(1)}, f32[256,512]{1,0:T(8,128)S(1)}, u32[]{:S(2)}, u32[]{:S(2)}) collective-permute-start(f32[256,512]{1,0:T(8,128)S(1)} %shard_map.47.refs_2_), channel_id=1, source_target_pairs={{0,56},{8,0},{16,8},{24,16},{32,24},{40,32},{48,40},{56,48},{1,57}... | collective-permute-start | bytes 1572872 | tf_op jit(solution)/shard_map/ppermute | solution.py:234
  22.4 8.2 %collective-permute-done.5.refs_2_.refs_5_ = f32[256,512]{1,0:T(8,128)S(1)} collective-permute-done((f32[256,512]{1,0:T(8,128)S(1)}, f32[256,512]{1,0:T(8,128)S(1)}, u32[]{:S(2)}, u32[]{:S(2)}) %collective-permute-start.5) | collective-permute-done | bytes 524320 | tf_op jit(solution)/shard_map/ppermute | solution.py:239
  30.6 2.6 %collective-permute-done.4.refs_1_ = f32[256,512]{1,0:T(8,128)S(1)} collective-permute-done((f32[256,512]{1,0:T(8,128)S(1)}, f32[256,512]{1,0:T(8,128)S(1)}, u32[]{:S(2)}, u32[]{:S(2)}) %collective-permute-start.4) | collective-permute-done | bytes 524320 | tf_op jit(solution)/shard_map/ppermute | solution.py:234
  33.2 3.1 %collective-permute-done.3.refs_0_ = f32[256,512]{1,0:T(8,128)S(1)} collective-permute-done((f32[256,512]{1,0:T(8,128)S(1)}, f32[256,512]{1,0:T(8,128)S(1)}, u32[]{:S(2)}, u32[]{:S(2)}) %collective-permute-start.3) | collective-permute-done | bytes 524320 | tf_op jit(solution)/shard_map/ppermute | solution.py:234
  37.4 2.7 %collective-permute-start.7 = (f32[256,512]{1,0:T(8,128)}, f32[256,512]{1,0:T(8,128)S(1)}, u32[]{:S(2)}, u32[]{:S(2)}) collective-permute-start(f32[256,512]{1,0:T(8,128)} %get-tuple-element.49.refs_4_), channel_id=1, source_target_pairs={{0,56},{8,0},{16,8},{24,16},{32,24},{40,32},{48,40},{56,48},{1,57}... | collective-permute-start | bytes 1572872 | tf_op jit(solution)/shard_map/ppermute | solution.py:234
  40.1 4.4 %shard_map.49 = (f32[512,512]{1,0:T(8,128)S(1)}, f32[8,128]{1,0:T(8,128)S(1)}) custom-call(s32[3]{0:T(128)S(1)} %pad_add_fusion.refs_0_, f32[512,4096]{1,0:T(8,128)} %refs_1_.11, f32[256,512]{1,0:T(8,128)S(1)} %shard_map.47.refs_2_, f32[256,512]{1,0:T(8,128)S(1)} %get-tuple-element.48.refs_3_, f32[256,512]{1,0:T(8,128)} %get-tuple-element.49.refs_4_, ...), custom_call_target="tpu_custom_call" | custom-call | flops 1610612736 | tf_op jit(solution)/shard_map/pallas_call | solution.py:105
  44.6 5.6 %collective-permute-done.6.refs_1_ = f32[256,512]{1,0:T(8,128)S(1)} collective-permute-done((f32[256,512]{1,0:T(8,128)S(1)}, f32[256,512]{1,0:T(8,128)S(1)}, u32[]{:S(2)}, u32[]{:S(2)}) %collective-permute-start.6) | collective-permute-done | bytes 524320 | tf_op jit(solution)/shard_map/ppermute | solution.py:234
  50.8 2.7 %collective-permute-start.11 = (f32[256,512]{1,0:T(8,128)S(1)}, f32[256,512]{1,0:T(8,128)S(1)}, u32[]{:S(2)}, u32[]{:S(2)}) collective-permute-start(f32[256,512]{1,0:T(8,128)S(1)} %get-tuple-element.52.refs_3_), channel_id=1, source_target_pairs={{0,56},{8,0},{16,8},{24,16},{32,24},{40,32},{48,40},{56,48},{1,57}... | collective-permute-start | bytes 1572872 | tf_op jit(solution)/shard_map/ppermute | solution.py:234
  53.5 2.2 %collective-permute-start.10 = (f32[256,512]{1,0:T(8,128)S(1)}, f32[256,512]{1,0:T(8,128)S(1)}, u32[]{:S(2)}, u32[]{:S(2)}) collective-permute-start(f32[256,512]{1,0:T(8,128)S(1)} %get-tuple-element.52.refs_3_), channel_id=1, source_target_pairs={{0,4},{4,0},{1,5},{5,1},{2,6},{6,2},{3,7},{7,3},{8,12},{12,8},{9,1... | collective-permute-start | bytes 1572872 | tf_op jit(solution)/shard_map/ppermute | solution.py:239
  55.7 3.3 %shard_map.51 = (f32[512,512]{1,0:T(8,128)S(1)}, f32[8,128]{1,0:T(8,128)S(1)}) custom-call(s32[3]{0:T(128)S(1)} %pad_add_fusion.refs_0_, f32[512,4096]{1,0:T(8,128)} %refs_1_.11, f32[256,512]{1,0:T(8,128)S(1)} %get-tuple-element.51.refs_2_.refs_3_, f32[256,512]{1,0:T(8,128)S(1)} %get-tuple-element.52.refs_3_, ...), custom_call_target="tpu_custom_call" | custom-call | flops 1207959552 | tf_op jit(solution)/shard_map/pallas_call | solution.py:105
  59.0 3.8 %collective-permute-done.9.refs_1_ = f32[256,512]{1,0:T(8,128)S(1)} collective-permute-done((f32[256,512]{1,0:T(8,128)S(1)}, f32[256,512]{1,0:T(8,128)S(1)}, u32[]{:S(2)}, u32[]{:S(2)}) %collective-permute-start.9) | collective-permute-done | bytes 524320 | tf_op jit(solution)/shard_map/ppermute | solution.py:234
  62.8 2.4 %collective-permute-done.10.refs_2_ = f32[256,512]{1,0:T(8,128)S(1)} collective-permute-done((f32[256,512]{1,0:T(8,128)S(1)}, f32[256,512]{1,0:T(8,128)S(1)}, u32[]{:S(2)}, u32[]{:S(2)}) %collective-permute-start.10) | collective-permute-done | bytes 524320 | tf_op jit(solution)/shard_map/ppermute | solution.py:239
  65.3 2.0 %collective-permute-start.12 = (f32[256,512]{1,0:T(8,128)S(1)}, f32[256,512]{1,0:T(8,128)S(1)}, u32[]{:S(2)}, u32[]{:S(2)}) collective-permute-start(f32[256,512]{1,0:T(8,128)S(1)} %get-tuple-element.59), channel_id=1, source_target_pairs={{0,4},{4,0},{1,5},{5,1},{2,6},{6,2},{3,7},{7,3},{8,12},{12,8},{9,1... | collective-permute-start | bytes 1572872 | tf_op jit(solution)/shard_map/ppermute | solution.py:239
  67.4 2.7 %collective-permute-start.13 = (f32[256,512]{1,0:T(8,128)S(1)}, f32[256,512]{1,0:T(8,128)S(1)}, u32[]{:S(2)}, u32[]{:S(2)}) collective-permute-start(f32[256,512]{1,0:T(8,128)S(1)} %get-tuple-element.56.refs_4_), channel_id=1, source_target_pairs={{0,56},{8,0},{16,8},{24,16},{32,24},{40,32},{48,40},{56,48},{1,57}... | collective-permute-start | bytes 1572872 | tf_op jit(solution)/shard_map/ppermute | solution.py:234
  70.0 3.3 %shard_map.53 = (f32[512,512]{1,0:T(8,128)S(1)}, f32[8,128]{1,0:T(8,128)S(1)}) custom-call(s32[3]{0:T(128)S(1)} %pad_add_fusion.refs_0_, f32[512,4096]{1,0:T(8,128)} %refs_1_.11, f32[256,512]{1,0:T(8,128)S(1)} %get-tuple-element.55.refs_2_, f32[256,512]{1,0:T(8,128)S(1)} %collective-permute-done.11.refs_4_.refs_3_, ...), custom_call_target="tpu_custom_call" | custom-call | flops 1207959552 | tf_op jit(solution)/shard_map/pallas_call | solution.py:105
  73.4 2.9 %collective-permute-done.12.refs_1_ = f32[256,512]{1,0:T(8,128)S(1)} collective-permute-done((f32[256,512]{1,0:T(8,128)S(1)}, f32[256,512]{1,0:T(8,128)S(1)}, u32[]{:S(2)}, u32[]{:S(2)}) %collective-permute-start.12) | collective-permute-done | bytes 524320 | tf_op jit(solution)/shard_map/ppermute | solution.py:239
  78.9 2.7 %collective-permute-start.16 = (f32[256,512]{1,0:T(8,128)S(1)}, f32[256,512]{1,0:T(8,128)S(1)}, u32[]{:S(2)}, u32[]{:S(2)}) collective-permute-start(f32[256,512]{1,0:T(8,128)S(1)} %get-tuple-element.61.refs_3_), channel_id=1, source_target_pairs={{0,56},{8,0},{16,8},{24,16},{32,24},{40,32},{48,40},{56,48},{1,57}... | collective-permute-start | bytes 1572872 | tf_op jit(solution)/shard_map/ppermute | solution.py:234
  81.6 3.3 %shard_map.55 = (f32[512,512]{1,0:T(8,128)S(1)}, f32[8,128]{1,0:T(8,128)}) custom-call(s32[3]{0:T(128)S(1)} %pad_add_fusion.refs_0_, f32[512,4096]{1,0:T(8,128)} %refs_1_.11, f32[256,512]{1,0:T(8,128)S(1)} %collective-permute-done.14.refs_4_.refs_2_, f32[256,512]{1,0:T(8,128)S(1)} %get-tuple-element.61.refs_3_, f32[256,512]{1,0:T(8,128)S(1)} %get-tuple-element.60.refs_4_, ...), custom_call_target="tpu_custom_call" | custom-call | flops 1207959552 | tf_op jit(solution)/shard_map/pallas_call | solution.py:105
  84.9 2.2 %collective-permute-done.17.refs_4_ = f32[256,512]{1,0:T(8,128)S(1)} collective-permute-done((f32[256,512]{1,0:T(8,128)S(1)}, f32[256,512]{1,0:T(8,128)S(1)}, u32[]{:S(2)}, u32[]{:S(2)}) %collective-permute-start.17) | collective-permute-done | bytes 524320 | tf_op jit(solution)/shard_map/ppermute | solution.py:239
  88.4 3.5 %shard_map.56 = (f32[64,512]{1,0:T(8,128)S(1)}, f32[64,512]{1,0:T(8,128)S(1)}, f32[64,512]{1,0:T(8,128)S(1)}, f32[64,512]{1,0:T(8,128)S(1)}, f32[64,512]{1,0:T(8...) custom-call(s32[3]{0:T(128)S(1)} %pad_add_fusion.refs_0_, f32[512,4096]{1,0:T(8,128)} %refs_1_.11, ...), custom_call_target="tpu_custom_call" | custom-call | flops 1207959552 | tf_op jit(solution)/shard_map/pallas_call | solution.py:105
  96.8 2.3 %collective-permute-start.23 = (f32[64,512]{1,0:T(8,128)S(1)}, f32[64,512]{1,0:T(8,128)S(1)}, u32[]{:S(2)}, u32[]{:S(2)}) collective-permute-start(f32[64,512]{1,0:T(8,128)S(1)} %get-tuple-element.72), channel_id=1, source_target_pairs={{0,3},{1,0},{2,1},{3,2},{4,7},{5,4},{6,5},{7,6},{8,11},{9,8},{10,9... | collective-permute-start | bytes 393224 | tf_op jit(solution)/shard_map/ppermute | solution.py:234
  100.2 3.0 %collective-permute-start.21 = (f32[64,512]{1,0:T(8,128)S(1)}, f32[64,512]{1,0:T(8,128)S(1)}, u32[]{:S(2)}, u32[]{:S(2)}) collective-permute-start(f32[64,512]{1,0:T(8,128)S(1)} %shard_map.57.refs_0_), channel_id=1, source_target_pairs={{0,32},{8,40},{16,48},{24,56},{32,0},{40,8},{48,16},{56,24},{1,33}... | collective-permute-start | bytes 393224 | tf_op jit(solution)/shard_map/ppermute | solution.py:234
  103.2 1.9 %collective-permute-done.24.refs_3_ = f32[64,512]{1,0:T(8,128)S(1)} collective-permute-done((f32[64,512]{1,0:T(8,128)S(1)}, f32[64,512]{1,0:T(8,128)S(1)}, u32[]{:S(2)}, u32[]{:S(2)}) %collective-permute-start.24) | collective-permute-done | bytes 131104 | tf_op jit(solution)/shard_map/ppermute | solution.py:234
  105.2 3.4 %collective-permute-start.25 = (f32[64,512]{1,0:T(8,128)S(1)}, f32[64,512]{1,0:T(8,128)S(1)}, u32[]{:S(2)}, u32[]{:S(2)}) collective-permute-start(f32[64,512]{1,0:T(8,128)S(1)} %shard_map.59.refs_0_), channel_id=1, source_target_pairs={{0,32},{8,40},{16,48},{24,56},{32,0},{40,8},{48,16},{56,24},{1,33}... | collective-permute-start | bytes 393224 | tf_op jit(solution)/shard_map/ppermute | solution.py:234
  108.7 10.5 %collective-permute-start.28 = (f32[16,512]{1,0:T(8,128)S(1)}, f32[16,512]{1,0:T(8,128)S(1)}, u32[]{:S(2)}, u32[]{:S(2)}) collective-permute-start(f32[16,512]{1,0:T(8,128)S(1)} %get-tuple-element.77), channel_id=1, source_target_pairs={{0,64},{1,65},{2,66},{3,67},{64,1},{65,0},{66,3},{67,2},{128,192},... | collective-permute-start | bytes 98312 | tf_op jit(solution)/shard_map/ppermute | solution.py:307
  119.2 2.2 %collective-permute-start.27 = (f32[8,512]{1,0:T(8,128)S(1)}, f32[8,512]{1,0:T(8,128)S(1)}, u32[]{:S(2)}, u32[]{:S(2)}) collective-permute-start(f32[8,512]{1,0:T(8,128)S(1)} %get-tuple-element.76), channel_id=1, source_target_pairs={{0,2},{1,3},{2,0},{3,1},{64,66},{65,67},{66,64},{67,65},{128,130},... | collective-permute-start | bytes 49160 | tf_op jit(solution)/shard_map/ppermute | solution.py:307
  123.3 2.8 %collective-permute-start.31 = (f32[16,512]{1,0:T(8,128)S(1)}, f32[16,512]{1,0:T(8,128)S(1)}, u32[]{:S(2)}, u32[]{:S(2)}) collective-permute-start(f32[16,512]{1,0:T(8,128)S(1)} %get-tuple-element.80), channel_id=1, source_target_pairs={{0,130},{1,131},{2,128},{3,129},{64,194},{65,195},{66,192},{67,193... | collective-permute-start | bytes 98312 | tf_op jit(solution)/shard_map/ppermute | solution.py:307
  126.9 2.2 %collective-permute-start.33 = (f32[16,512]{1,0:T(8,128)S(1)}, f32[16,512]{1,0:T(8,128)S(1)}, u32[]{:S(2)}, u32[]{:S(2)}) collective-permute-start(f32[16,512]{1,0:T(8,128)S(1)} %get-tuple-element.82), channel_id=1, source_target_pairs={{0,194},{1,195},{2,192},{3,193},{64,130},{65,131},{66,128},{67,129... | collective-permute-start | bytes 98312 | tf_op jit(solution)/shard_map/ppermute | solution.py:307
  (59 shorter events, 24.0 us)
Async XLA Ops:
  4.3 5.1 %collective-permute-start = (f32[256,128]{1,0:T(8,128)S(1)}, f32[256,128]{1,0:T(8,128)S(1)}, u32[]{:S(2)}, u32[]{:S(2)}) collective-permute-start(f32[256,128]{1,0:T(8,128)S(1)} %get-tuple-element.45), channel_id=1, source_target_pairs={{0,64},{64,0},{128,192},{192,128},{1,65},{65,1},{129,193},{193,129... | collective-permute-start | bytes 393224 | tf_op jit(solution)/shard_map/ppermute | solution.py:239
  7.6 5.1 %collective-permute-start.1 = (f32[256,128]{1,0:T(8,128)S(1)}, f32[256,128]{1,0:T(8,128)S(1)}, u32[]{:S(2)}, u32[]{:S(2)}) collective-permute-start(f32[256,128]{1,0:T(8,128)S(1)} %get-tuple-element.46), channel_id=1, source_target_pairs={{0,128},{64,192},{128,0},{192,64},{1,129},{65,193},{129,1},{193,65... | collective-permute-start | bytes 393224 | tf_op jit(solution)/shard_map/ppermute | solution.py:239
  7.6 8.0 %collective-permute-start.2 = (f32[256,128]{1,0:T(8,128)S(1)}, f32[256,128]{1,0:T(8,128)S(1)}, u32[]{:S(2)}, u32[]{:S(2)}) collective-permute-start(f32[256,128]{1,0:T(8,128)S(1)} %get-tuple-element.47), channel_id=1, source_target_pairs={{0,192},{64,128},{128,64},{192,0},{1,193},{65,129},{129,65},{193,1... | collective-permute-start | bytes 393224 | tf_op jit(solution)/shard_map/ppermute | solution.py:239
  15.7 14.9 %collective-permute-start.5 = (f32[256,512]{1,0:T(8,128)S(1)}, f32[256,512]{1,0:T(8,128)S(1)}, u32[]{:S(2)}, u32[]{:S(2)}) collective-permute-start(f32[256,512]{1,0:T(8,128)S(1)} %shard_map.47.refs_2_), channel_id=1, source_target_pairs={{0,4},{4,0},{1,5},{5,1},{2,6},{6,2},{3,7},{7,3},{8,12},{12,8},{9,1... | collective-permute-start | bytes 1572872 | tf_op jit(solution)/shard_map/ppermute | solution.py:239
  16.8 16.4 %collective-permute-start.4 = (f32[256,512]{1,0:T(8,128)S(1)}, f32[256,512]{1,0:T(8,128)S(1)}, u32[]{:S(2)}, u32[]{:S(2)}) collective-permute-start(f32[256,512]{1,0:T(8,128)S(1)} %shard_map.47.refs_2_), channel_id=1, source_target_pairs={{0,56},{8,0},{16,8},{24,16},{32,24},{40,32},{48,40},{56,48},{1,57}... | collective-permute-start | bytes 1572872 | tf_op jit(solution)/shard_map/ppermute | solution.py:234
  22.4 13.9 %collective-permute-start.3 = (f32[256,512]{1,0:T(8,128)S(1)}, f32[256,512]{1,0:T(8,128)S(1)}, u32[]{:S(2)}, u32[]{:S(2)}) collective-permute-start(f32[256,512]{1,0:T(8,128)S(1)} %shard_map.47.refs_2_), channel_id=1, source_target_pairs={{0,8},{8,16},{16,24},{24,32},{32,40},{40,48},{48,56},{56,0},{1,9},... | collective-permute-start | bytes 1572872 | tf_op jit(solution)/shard_map/ppermute | solution.py:234
  37.2 13.0 %collective-permute-start.6 = (f32[256,512]{1,0:T(8,128)S(1)}, f32[256,512]{1,0:T(8,128)S(1)}, u32[]{:S(2)}, u32[]{:S(2)}) collective-permute-start(f32[256,512]{1,0:T(8,128)S(1)} %get-tuple-element.48.refs_3_), channel_id=1, source_target_pairs={{0,8},{8,16},{16,24},{24,32},{32,40},{40,48},{48,56},{56,0},{1,9},... | collective-permute-start | bytes 1572872 | tf_op jit(solution)/shard_map/ppermute | solution.py:234
  37.2 13.5 %collective-permute-start.8 = (f32[256,512]{1,0:T(8,128)}, f32[256,512]{1,0:T(8,128)S(1)}, u32[]{:S(2)}, u32[]{:S(2)}) collective-permute-start(f32[256,512]{1,0:T(8,128)} %get-tuple-element.49.refs_4_), channel_id=1, source_target_pairs={{0,4},{4,0},{1,5},{5,1},{2,6},{6,2},{3,7},{7,3},{8,12},{12,8},{9,1... | collective-permute-start | bytes 1572872 | tf_op jit(solution)/shard_map/ppermute | solution.py:239
  37.4 13.2 %collective-permute-start.7 = (f32[256,512]{1,0:T(8,128)}, f32[256,512]{1,0:T(8,128)S(1)}, u32[]{:S(2)}, u32[]{:S(2)}) collective-permute-start(f32[256,512]{1,0:T(8,128)} %get-tuple-element.49.refs_4_), channel_id=1, source_target_pairs={{0,56},{8,0},{16,8},{24,16},{32,24},{40,32},{48,40},{56,48},{1,57}... | collective-permute-start | bytes 1572872 | tf_op jit(solution)/shard_map/ppermute | solution.py:234
  50.7 12.1 %collective-permute-start.9 = (f32[256,512]{1,0:T(8,128)S(1)}, f32[256,512]{1,0:T(8,128)S(1)}, u32[]{:S(2)}, u32[]{:S(2)}) collective-permute-start(f32[256,512]{1,0:T(8,128)S(1)} %get-tuple-element.51.refs_2_.refs_3_), channel_id=1, source_target_pairs={{0,8},{8,16},{16,24},{24,32},{32,40},{40,48},{48,56},{56,0},{1,9},... | collective-permute-start | bytes 1572872 | tf_op jit(solution)/shard_map/ppermute | solution.py:234
  50.8 12.0 %collective-permute-start.11 = (f32[256,512]{1,0:T(8,128)S(1)}, f32[256,512]{1,0:T(8,128)S(1)}, u32[]{:S(2)}, u32[]{:S(2)}) collective-permute-start(f32[256,512]{1,0:T(8,128)S(1)} %get-tuple-element.52.refs_3_), channel_id=1, source_target_pairs={{0,56},{8,0},{16,8},{24,16},{32,24},{40,32},{48,40},{56,48},{1,57}... | collective-permute-start | bytes 1572872 | tf_op jit(solution)/shard_map/ppermute | solution.py:234
  53.5 11.8 %collective-permute-start.10 = (f32[256,512]{1,0:T(8,128)S(1)}, f32[256,512]{1,0:T(8,128)S(1)}, u32[]{:S(2)}, u32[]{:S(2)}) collective-permute-start(f32[256,512]{1,0:T(8,128)S(1)} %get-tuple-element.52.refs_3_), channel_id=1, source_target_pairs={{0,4},{4,0},{1,5},{5,1},{2,6},{6,2},{3,7},{7,3},{8,12},{12,8},{9,1... | collective-permute-start | bytes 1572872 | tf_op jit(solution)/shard_map/ppermute | solution.py:239
  65.3 10.9 %collective-permute-start.12 = (f32[256,512]{1,0:T(8,128)S(1)}, f32[256,512]{1,0:T(8,128)S(1)}, u32[]{:S(2)}, u32[]{:S(2)}) collective-permute-start(f32[256,512]{1,0:T(8,128)S(1)} %get-tuple-element.59), channel_id=1, source_target_pairs={{0,4},{4,0},{1,5},{5,1},{2,6},{6,2},{3,7},{7,3},{8,12},{12,8},{9,1... | collective-permute-start | bytes 1572872 | tf_op jit(solution)/shard_map/ppermute | solution.py:239
  67.3 10.0 %collective-permute-start.14 = (f32[256,512]{1,0:T(8,128)S(1)}, f32[256,512]{1,0:T(8,128)S(1)}, u32[]{:S(2)}, u32[]{:S(2)}) collective-permute-start(f32[256,512]{1,0:T(8,128)S(1)} %get-tuple-element.55.refs_2_), channel_id=1, source_target_pairs={{0,8},{8,16},{16,24},{24,32},{32,40},{40,48},{48,56},{56,0},{1,9},... | collective-permute-start | bytes 1572872 | tf_op jit(solution)/shard_map/ppermute | solution.py:234
  67.4 10.0 %collective-permute-start.13 = (f32[256,512]{1,0:T(8,128)S(1)}, f32[256,512]{1,0:T(8,128)S(1)}, u32[]{:S(2)}, u32[]{:S(2)}) collective-permute-start(f32[256,512]{1,0:T(8,128)S(1)} %get-tuple-element.56.refs_4_), channel_id=1, source_target_pairs={{0,56},{8,0},{16,8},{24,16},{32,24},{40,32},{48,40},{56,48},{1,57}... | collective-permute-start | bytes 1572872 | tf_op jit(solution)/shard_map/ppermute | solution.py:234
  77.5 9.6 %collective-permute-start.17 = (f32[256,512]{1,0:T(8,128)S(1)}, f32[256,512]{1,0:T(8,128)S(1)}, u32[]{:S(2)}, u32[]{:S(2)}) collective-permute-start(f32[256,512]{1,0:T(8,128)S(1)} %get-tuple-element.62), channel_id=1, source_target_pairs={{0,4},{4,0},{1,5},{5,1},{2,6},{6,2},{3,7},{7,3},{8,12},{12,8},{9,1... | collective-permute-start | bytes 1572872 | tf_op jit(solution)/shard_map/ppermute | solution.py:239
  78.9 9.5 %collective-permute-start.15 = (f32[256,512]{1,0:T(8,128)S(1)}, f32[256,512]{1,0:T(8,128)S(1)}, u32[]{:S(2)}, u32[]{:S(2)}) collective-permute-start(f32[256,512]{1,0:T(8,128)S(1)} %get-tuple-element.60.refs_4_), channel_id=1, source_target_pairs={{0,8},{8,16},{16,24},{24,32},{32,40},{40,48},{48,56},{56,0},{1,9},... | collective-permute-start | bytes 1572872 | tf_op jit(solution)/shard_map/ppermute | solution.py:234
  78.9 9.5 %collective-permute-start.16 = (f32[256,512]{1,0:T(8,128)S(1)}, f32[256,512]{1,0:T(8,128)S(1)}, u32[]{:S(2)}, u32[]{:S(2)}) collective-permute-start(f32[256,512]{1,0:T(8,128)S(1)} %get-tuple-element.61.refs_3_), channel_id=1, source_target_pairs={{0,56},{8,0},{16,8},{24,16},{32,24},{40,32},{48,40},{56,48},{1,57}... | collective-permute-start | bytes 1572872 | tf_op jit(solution)/shard_map/ppermute | solution.py:234
  92.0 7.1 %collective-permute-start.18 = (f32[64,512]{1,0:T(8,128)S(1)}, f32[64,512]{1,0:T(8,128)S(1)}, u32[]{:S(2)}, u32[]{:S(2)}) collective-permute-start(f32[64,512]{1,0:T(8,128)S(1)} %get-tuple-element.66), channel_id=1, source_target_pairs={{0,1},{1,2},{2,3},{3,0},{4,5},{5,6},{6,7},{7,4},{8,9},{9,10},{10,1... | collective-permute-start | bytes 393224 | tf_op jit(solution)/shard_map/ppermute | solution.py:234
  93.3 6.0 %collective-permute-start.19 = (f32[64,512]{1,0:T(8,128)S(1)}, f32[64,512]{1,0:T(8,128)S(1)}, u32[]{:S(2)}, u32[]{:S(2)}) collective-permute-start(f32[64,512]{1,0:T(8,128)S(1)} %get-tuple-element.67), channel_id=1, source_target_pairs={{0,3},{1,0},{2,1},{3,2},{4,7},{5,4},{6,5},{7,6},{8,11},{9,8},{10,9... | collective-permute-start | bytes 393224 | tf_op jit(solution)/shard_map/ppermute | solution.py:234
  94.9 5.3 %collective-permute-start.20 = (f32[64,512]{1,0:T(8,128)S(1)}, f32[64,512]{1,0:T(8,128)S(1)}, u32[]{:S(2)}, u32[]{:S(2)}) collective-permute-start(f32[64,512]{1,0:T(8,128)S(1)} %get-tuple-element.68), channel_id=1, source_target_pairs={{0,2},{1,3},{2,0},{3,1},{4,6},{5,7},{6,4},{7,5},{8,10},{9,11},{10,... | collective-permute-start | bytes 393224 | tf_op jit(solution)/shard_map/ppermute | solution.py:234
  96.4 6.8 %collective-permute-start.22 = (f32[64,512]{1,0:T(8,128)S(1)}, f32[64,512]{1,0:T(8,128)S(1)}, u32[]{:S(2)}, u32[]{:S(2)}) collective-permute-start(f32[64,512]{1,0:T(8,128)S(1)} %get-tuple-element.71), channel_id=1, source_target_pairs={{0,1},{1,2},{2,3},{3,0},{4,5},{5,6},{6,7},{7,4},{8,9},{9,10},{10,1... | collective-permute-start | bytes 393224 | tf_op jit(solution)/shard_map/ppermute | solution.py:234
  96.8 6.4 %collective-permute-start.23 = (f32[64,512]{1,0:T(8,128)S(1)}, f32[64,512]{1,0:T(8,128)S(1)}, u32[]{:S(2)}, u32[]{:S(2)}) collective-permute-start(f32[64,512]{1,0:T(8,128)S(1)} %get-tuple-element.72), channel_id=1, source_target_pairs={{0,3},{1,0},{2,1},{3,2},{4,7},{5,4},{6,5},{7,6},{8,11},{9,8},{10,9... | collective-permute-start | bytes 393224 | tf_op jit(solution)/shard_map/ppermute | solution.py:234
  99.1 6.0 %collective-permute-start.24 = (f32[64,512]{1,0:T(8,128)S(1)}, f32[64,512]{1,0:T(8,128)S(1)}, u32[]{:S(2)}, u32[]{:S(2)}) collective-permute-start(f32[64,512]{1,0:T(8,128)S(1)} %get-tuple-element.73), channel_id=1, source_target_pairs={{0,2},{1,3},{2,0},{3,1},{4,6},{5,7},{6,4},{7,5},{8,10},{9,11},{10,... | collective-permute-start | bytes 393224 | tf_op jit(solution)/shard_map/ppermute | solution.py:234
  100.2 8.3 %collective-permute-start.21 = (f32[64,512]{1,0:T(8,128)S(1)}, f32[64,512]{1,0:T(8,128)S(1)}, u32[]{:S(2)}, u32[]{:S(2)}) collective-permute-start(f32[64,512]{1,0:T(8,128)S(1)} %shard_map.57.refs_0_), channel_id=1, source_target_pairs={{0,32},{8,40},{16,48},{24,56},{32,0},{40,8},{48,16},{56,24},{1,33}... | collective-permute-start | bytes 393224 | tf_op jit(solution)/shard_map/ppermute | solution.py:234
  105.2 16.7 %collective-permute-start.25 = (f32[64,512]{1,0:T(8,128)S(1)}, f32[64,512]{1,0:T(8,128)S(1)}, u32[]{:S(2)}, u32[]{:S(2)}) collective-permute-start(f32[64,512]{1,0:T(8,128)S(1)} %shard_map.59.refs_0_), channel_id=1, source_target_pairs={{0,32},{8,40},{16,48},{24,56},{32,0},{40,8},{48,16},{56,24},{1,33}... | collective-permute-start | bytes 393224 | tf_op jit(solution)/shard_map/ppermute | solution.py:234
  108.6 17.5 %collective-permute-start.26 = (f32[16,512]{1,0:T(8,128)S(1)}, f32[16,512]{1,0:T(8,128)S(1)}, u32[]{:S(2)}, u32[]{:S(2)}) collective-permute-start(f32[16,512]{1,0:T(8,128)S(1)} %get-tuple-element.75), channel_id=1, source_target_pairs={{0,1},{1,2},{2,3},{3,0},{64,65},{65,66},{66,67},{67,64},{128,129},... | collective-permute-start | bytes 98312 | tf_op jit(solution)/shard_map/ppermute | solution.py:307
  108.7 18.2 %collective-permute-start.28 = (f32[16,512]{1,0:T(8,128)S(1)}, f32[16,512]{1,0:T(8,128)S(1)}, u32[]{:S(2)}, u32[]{:S(2)}) collective-permute-start(f32[16,512]{1,0:T(8,128)S(1)} %get-tuple-element.77), channel_id=1, source_target_pairs={{0,64},{1,65},{2,66},{3,67},{64,1},{65,0},{66,3},{67,2},{128,192},... | collective-permute-start | bytes 98312 | tf_op jit(solution)/shard_map/ppermute | solution.py:307
  121.4 7.7 %collective-permute-start.29 = (f32[16,512]{1,0:T(8,128)S(1)}, f32[16,512]{1,0:T(8,128)S(1)}, u32[]{:S(2)}, u32[]{:S(2)}) collective-permute-start(f32[16,512]{1,0:T(8,128)S(1)} %get-tuple-element.78), channel_id=1, source_target_pairs={{0,66},{1,67},{2,64},{3,65},{64,3},{65,2},{66,1},{67,0},{128,194},... | collective-permute-start | bytes 98312 | tf_op jit(solution)/shard_map/ppermute | solution.py:307
  121.9 7.2 %collective-permute-start.30 = (f32[16,512]{1,0:T(8,128)S(1)}, f32[16,512]{1,0:T(8,128)S(1)}, u32[]{:S(2)}, u32[]{:S(2)}) collective-permute-start(f32[16,512]{1,0:T(8,128)S(1)} %get-tuple-element.79), channel_id=1, source_target_pairs={{0,128},{1,129},{2,130},{3,131},{64,192},{65,193},{66,194},{67,195... | collective-permute-start | bytes 98312 | tf_op jit(solution)/shard_map/ppermute | solution.py:307
  123.3 5.8 %collective-permute-start.31 = (f32[16,512]{1,0:T(8,128)S(1)}, f32[16,512]{1,0:T(8,128)S(1)}, u32[]{:S(2)}, u32[]{:S(2)}) collective-permute-start(f32[16,512]{1,0:T(8,128)S(1)} %get-tuple-element.80), channel_id=1, source_target_pairs={{0,130},{1,131},{2,128},{3,129},{64,194},{65,195},{66,192},{67,193... | collective-permute-start | bytes 98312 | tf_op jit(solution)/shard_map/ppermute | solution.py:307
  126.9 5.5 %collective-permute-start.33 = (f32[16,512]{1,0:T(8,128)S(1)}, f32[16,512]{1,0:T(8,128)S(1)}, u32[]{:S(2)}, u32[]{:S(2)}) collective-permute-start(f32[16,512]{1,0:T(8,128)S(1)} %get-tuple-element.82), channel_id=1, source_target_pairs={{0,194},{1,195},{2,192},{3,193},{64,130},{65,131},{66,128},{67,129... | collective-permute-start | bytes 98312 | tf_op jit(solution)/shard_map/ppermute | solution.py:307
  (5 other events, 58.1 us)
